TPU v7x, 32 devices: a whole 2x2x4 slice. The times are simulated.
32 devices in a mesh: row: 4 (over x, core), col: 4 (over z), depth: 2 (over y).
Axes of the slice: x: 2, y: 2, z: 4, core: 2. Of those that a mesh axis runs over, the one named last changes fastest.
Arguments:
- a_blocks: float32 [128, 8, 64, 128], P(('row', 'col', 'depth')), may hold values from -0.9 to 0.9
- a_index: int32 [128, 8, 2], P(('row', 'col', 'depth')), may hold values from 0 to 255, as said below
- b_blocks: float32 [2048, 4, 64, 256], P(('row', 'depth'), 'col'), may hold values from -0.9 to 0.9
- b_index: int32 [2048, 4, 4], P(('row', 'depth'), 'col'), may hold values from 0 to 511, as said below
- c_index: int32 [128, 4, 6], P('row', 'col'), may hold values from 0 to 511, as said below
Outputs:
- c_blocks: float32 [128, 4, 64, 384], P(('row', 'depth'), 'col')
Inputs may be any that keep to these rules, and one draw needn't show every extreme that they name: The pattern is banded: a_index[i, q, s] differs by at most 1 from (2048 * i // 128) // 8, and is clipped to the slab. The pattern is banded: for the row p of b_blocks, whose block row of B is h = (p % 256) * 8 + p // 256, b_index[p, c, b] differs by at most 2 from h // 4, and is clipped to the column tile. The pattern is banded: c_index[i, c, k] differs by at most 4 from (2048 * i // 128) // 4, and is clipped to the column tile.
All inputs are finite; a program needn't handle non-finite values.
Results may differ from a plain program's by a relative error of at most 0.0003.
Values sent between devices are 32-bit elements; how exact they have to be, the bound alone decides.
No kernel may reach another device: no remote copies, remote signals or barrier semaphores. Data moves between devices by JAX's collectives and lax.ppermute only.
A program may use at most 128 MiB of HBM per device.

v0:
```python
import jax
import jax.numpy as jnp
from jax import lax
from jax.sharding import PartitionSpec as P


def passed_along(value, axis, by):
    length = lax.axis_size(axis)
    return lax.ppermute(value, axis, [(i, (i + by) % length) for i in range(length)])


def contribute(total, a_vals, a_slots, b_vals, b_slots, c_slots):
    rows_here, block_size, a_width = a_vals.shape
    slot_count = a_slots.shape[1]
    b_count = b_slots.shape[1]
    picked = jnp.take(b_vals, a_slots, axis=0)
    picked_cols = jnp.take(b_slots, a_slots, axis=0)
    matches = (picked_cols[:, :, :, None] == c_slots[:, None, None, :]).astype(jnp.float32)
    a_parts = a_vals.reshape(rows_here, block_size, slot_count, block_size)
    products = jnp.einsum("rmsj,rsjn->rmsn", a_parts, picked, precision=lax.Precision.HIGHEST)
    products = products.reshape(rows_here, block_size, slot_count, b_count, block_size)
    placed = jnp.einsum("rmsbq,rsbk->rmkq", products, matches, precision=lax.Precision.HIGHEST)
    return total + placed.reshape(rows_here, block_size, -1)


def on_device(a_blocks, a_index, b_blocks, b_index, c_index):
    row_count = lax.axis_size("row")
    col_count = lax.axis_size("col")
    depth_count = lax.axis_size("depth")
    rows_dev, slab_total, block_size, a_width = a_blocks.shape
    slot_count = a_index.shape[2]
    grouped = a_blocks.reshape(rows_dev, col_count, depth_count, block_size, a_width)
    group_slots = a_index.reshape(rows_dev, col_count, depth_count, slot_count)
    parted, parted_slots = (
        lax.all_to_all(grouped, "depth", split_axis=2, concat_axis=0, tiled=True),
        lax.all_to_all(group_slots, "depth", split_axis=2, concat_axis=0, tiled=True),
    )
    parted = parted.reshape(-1, col_count, block_size, a_width)
    parted_slots = parted_slots.reshape(-1, col_count, slot_count)
    a_full, a_full_slots = (
        lax.all_gather(parted, "col", axis=0, tiled=True),
        lax.all_gather(parted_slots, "col", axis=0, tiled=True),
    )
    b_local = b_blocks[:, 0]
    b_local_slots = b_index[:, 0]
    c_slots = c_index[:, 0]
    layer_rows = parted.shape[0] * col_count
    row_index = lax.axis_index("row")
    total = jnp.zeros((layer_rows, block_size, c_slots.shape[1] * block_size), jnp.float32)
    b_now = b_local
    b_now_slots = b_local_slots
    for position in range(row_count):
        tile_now = (row_index + position) % row_count
        a_now = lax.dynamic_index_in_dim(a_full, tile_now, 1, keepdims=False)
        a_now_slots = lax.dynamic_index_in_dim(a_full_slots, tile_now, 1, keepdims=False)
        total = contribute(total, a_now, a_now_slots, b_now, b_now_slots, c_slots)
        if position + 1 < row_count:
            b_now, b_now_slots = passed_along((b_now, b_now_slots), "row", -1)
    partial_sums = total.reshape(total.shape[0], 1, block_size, total.shape[2])
    return lax.psum_scatter(partial_sums, "depth", scatter_dimension=0, tiled=True)


def solution(mesh):
    return jax.shard_map(
        on_device,
        mesh=mesh,
        in_specs=(
            P(("row", "col", "depth"), None, None, None),
            P(("row", "col", "depth"), None, None),
            P(("row", "depth"), "col", None, None),
            P(("row", "depth"), "col", None),
            P("row", "col", None),
        ),
        out_specs=P(("row", "depth"), "col", None, None),
        check_vma=False,
    )
```

profile of v0, /device:TPU:0, one launch (start us, length us, event | category | flops | bytes accessed | tf_op | source)
XLA Modules:
  0.0 784.9 jit_solution(10578903329876971286)
XLA Ops:
  9.0 181.2 %collective-permute-done.1 = f32[256,64,256]{2,1,0:T(8,128)S(1)} collective-permute-done((f32[256,64,256]{2,1,0:T(8,128)}, f32[256,64,256]{2,1,0:T(8,128)S(1)}, u32[]{:S(2)}, u32[]{:S(2)}) %collective-permute-start.1) | collective-permute-done | bytes 16777248 | tf_op jit(solution)/shard_map/ppermute | solution.py:9
  191.9 180.8 %collective-permute-done.3 = f32[256,64,256]{2,1,0:T(8,128)} collective-permute-done((f32[256,64,256]{2,1,0:T(8,128)S(1)}, f32[256,64,256]{2,1,0:T(8,128)}, u32[]{:S(2)}, u32[]{:S(2)}) %collective-permute-start.3) | collective-permute-done | bytes 16777248 | tf_op jit(solution)/shard_map/ppermute | solution.py:9
  376.1 16.2 %all_to_all.30 = f32[4,4,2,64,128]{4,3,1,0,2:T(8,128)} all-to-all(f32[4,4,2,64,128]{4,3,1,0,2:T(8,128)S(1)} %copy.105), channel_id=1, replica_groups=mesh['row'=4,'col'=4,'depth'=2] {'depth'}, dimensions={2} | all-to-all | bytes 2097152 | tf_op jit(solution)/shard_map/all_to_all | solution.py:35
  400.2 13.6 %all_gather.6 = s32[32,4,2]{1,2,0:T(2,128)S(1)} all-gather(s32[8,4,2]{1,2,0:T(2,128)S(1)} %bitcast.149), channel_id=1, replica_groups=mesh['row'=4,'col'=4,'depth'=2] {'col'}, dimensions={0}, use_global_device_ids=true | all-gather | bytes 1280 | tf_op jit(solution)/shard_map/all_gather | solution.py:42
  416.1 8.7 %gather_fusion.1 = f32[64,64,256]{2,1,0:T(8,128)} fusion(f32[256,64,256]{2,1,0:T(8,128)} %bitcast.143, s32[1024]{0:T(1024)S(1)} %pad_clamp_fusion.3), kind=kCustom, calls=%fused_computation.1.clone | custom fusion | bytes 8388864 | tf_op jit(solution)/shard_map/jit(_take)/gather | solution.py:16
  425.2 132.1 %collective-permute-done = s32[256,4]{1,0:T(8,128)S(1)} collective-permute-done((s32[256,4]{1,0:T(8,128)S(1)}, s32[256,4]{1,0:T(8,128)S(1)}, u32[]{:S(2)}, u32[]{:S(2)}) %collective-permute-start) | collective-permute-done | bytes 4128 | tf_op jit(solution)/shard_map/ppermute | solution.py:9
  567.3 4.0 constant_dynamic-slice_fusion
  583.1 9.1 %fusion.9 = f32[32,64,2,256]{3,1,2,0:T(8,128)} fusion(f32[32,2,64,256]{3,2,1,0:T(8,128)} %bitcast.131, f32[32,64,2,64]{3,2,1,0:T(2,128)} %reshape.106, pred[32,2]{1,0:T(8,128)(4,1)S(1)} %copy.99), kind=kOutput, calls=%fused_computation.20 | convolution fusion | flops 806354944 | bytes 9437248 | tf_op jit(solution)/shard_map/rmsj,rsjn->rmsn/dot_general | solution.py:20
  592.2 8.0 %reshape.107 = f32[32,64,2,4,64]{4,3,1,2,0:T(4,128)} reshape(f32[32,64,2,256]{3,1,2,0:T(8,128)} %fusion.9) | data formatting | bytes 8388608 | tf_op jit(solution)/shard_map/reshape | solution.py:21
  600.2 10.8 %fusion.38 = f32[32,6,64,64,1]{3,1,2,4,0:T(8,128)} fusion(f32[32,64,2,4,64]{4,3,1,2,0:T(4,128)} %reshape.107, s32[32,6]{1,0:T(8,128)S(1)} %bitcast.136, s32[32,2,4]{2,1,0:T(2,128)S(1)} %broadcast_select_fusion.3), kind=kOutput, calls=%fused_computation.41 | convolution fusion | flops 75499008 | bytes 7341824 | tf_op jit(solution)/shard_map/rmsbq,rsbk->rmkq/dot_general | solution.py:22
  611.0 8.5 %gather_fusion.3 = f32[64,64,256]{2,1,0:T(8,128)} fusion(f32[256,64,256]{2,1,0:T(8,128)} %copy-done, s32[1024]{0:T(1024)S(1)} %pad_clamp_fusion.2), kind=kCustom, calls=%fused_computation.5.clone | custom fusion | bytes 8388864 | tf_op jit(solution)/shard_map/jit(_take)/gather | solution.py:16
  619.5 9.2 %fusion.12 = f32[32,64,2,256]{3,1,2,0:T(8,128)} fusion(f32[32,2,64,256]{3,2,1,0:T(8,128)} %bitcast.132, f32[32,64,2,64]{3,2,1,0:T(2,128)} %reshape.108, pred[32,2]{1,0:T(8,128)(4,1)S(1)} %copy.109), kind=kOutput, calls=%fused_computation.21 | convolution fusion | flops 806354944 | bytes 9437248 | tf_op jit(solution)/shard_map/rmsj,rsjn->rmsn/dot_general | solution.py:20
  628.8 8.1 %reshape.109 = f32[32,64,2,4,64]{4,3,1,2,0:T(4,128)} reshape(f32[32,64,2,256]{3,1,2,0:T(8,128)} %fusion.12) | data formatting | bytes 8388608 | tf_op jit(solution)/shard_map/reshape | solution.py:21
  636.8 10.8 %fusion.36 = f32[32,6,64,64,1]{3,1,2,4,0:T(8,128)} fusion(f32[32,64,2,4,64]{4,3,1,2,0:T(4,128)} %reshape.109, s32[32,2,4]{2,1,0:T(2,128)S(1)} %broadcast_select_fusion.2, s32[32,6]{1,0:T(8,128)S(1)} %bitcast.137), kind=kOutput, calls=%fused_computation.39 | convolution fusion | flops 75499008 | bytes 7341824 | tf_op jit(solution)/shard_map/rmsbq,rsbk->rmkq/dot_general | solution.py:22
  647.7 8.5 %gather_fusion.5 = f32[64,64,256]{2,1,0:T(8,128)} fusion(f32[256,64,256]{2,1,0:T(8,128)} %collective-permute-done.3, s32[1024]{0:T(1024)S(1)} %pad_clamp_fusion.1), kind=kCustom, calls=%fused_computation.6.clone | custom fusion | bytes 8388864 | tf_op jit(solution)/shard_map/jit(_take)/gather | solution.py:16
  656.2 9.1 %fusion.15 = f32[32,64,2,256]{3,1,2,0:T(8,128)} fusion(f32[32,2,64,256]{3,2,1,0:T(8,128)} %bitcast.134, f32[32,64,2,64]{3,2,1,0:T(2,128)} %reshape.110, pred[32,2]{1,0:T(8,128)(4,1)S(1)} %copy.116), kind=kOutput, calls=%fused_computation.22 | convolution fusion | flops 806354944 | bytes 9437248 | tf_op jit(solution)/shard_map/rmsj,rsjn->rmsn/dot_general | solution.py:20
  665.3 8.0 %reshape.111 = f32[32,64,2,4,64]{4,3,1,2,0:T(4,128)} reshape(f32[32,64,2,256]{3,1,2,0:T(8,128)} %fusion.15) | data formatting | bytes 8388608 | tf_op jit(solution)/shard_map/reshape | solution.py:21
  673.3 10.8 %fusion.34 = f32[32,6,64,64,1]{3,1,2,4,0:T(8,128)} fusion(f32[32,64,2,4,64]{4,3,1,2,0:T(4,128)} %reshape.111, s32[32,2,4]{2,1,0:T(2,128)S(1)} %broadcast_select_fusion.1, s32[32,6]{1,0:T(8,128)S(1)} %bitcast.138), kind=kOutput, calls=%fused_computation.37 | convolution fusion | flops 75499008 | bytes 7341824 | tf_op jit(solution)/shard_map/rmsbq,rsbk->rmkq/dot_general | solution.py:22
  684.1 8.5 %gather_fusion.7 = f32[64,64,256]{2,1,0:T(8,128)} fusion(f32[256,64,256]{2,1,0:T(8,128)} %collective-permute-done.5, s32[1024]{0:T(1024)S(1)} %pad_clamp_fusion), kind=kCustom, calls=%fused_computation.7.clone | custom fusion | bytes 8388864 | tf_op jit(solution)/shard_map/jit(_take)/gather | solution.py:16
  692.7 8.5 %fusion.18 = f32[32,64,2,256]{3,1,2,0:T(8,128)} fusion(f32[32,2,64,256]{3,2,1,0:T(8,128)} %bitcast.133, f32[32,64,2,64]{3,2,1,0:T(2,128)S(1)} %reshape.112, pred[32,2]{1,0:T(8,128)(4,1)S(1)} %copy.123), kind=kOutput, calls=%fused_computation.23 | convolution fusion | flops 806354944 | bytes 9437248 | tf_op jit(solution)/shard_map/rmsj,rsjn->rmsn/dot_general | solution.py:20
  701.1 8.1 %reshape.113 = f32[32,64,2,4,64]{4,3,1,2,0:T(4,128)} reshape(f32[32,64,2,256]{3,1,2,0:T(8,128)} %fusion.18) | data formatting | bytes 8388608 | tf_op jit(solution)/shard_map/reshape | solution.py:21
  709.2 16.2 %fusion = f32[32,64,6,64]{3,2,1,0:T(8,128)} fusion(f32[32,6,64,64,1]{3,1,2,4,0:T(8,128)} %fusion.34, f32[32,6,64,64,1]{3,1,2,4,0:T(8,128)} %fusion.36, f32[32,6,64,64,1]{3,1,2,4,0:T(8,128)} %fusion.38, f32[32,64,2,4,64]{4,3,1,2,0:T(4,128)} %reshape.113, s32[32,2,4]{2,1,0:T(2,128)S(1)} %broadcast_select_fusion, s32[32,6]{1,0:T(8,128)S(1)} %bitcast.139), kind=kOutput, calls=%fused_computation.9 | convolution fusion | flops 77858304 | bytes 16779008 | tf_op jit(solution)/shard_map/rmsbq,rsbk->rmkq/dot_general | solution.py:22
  725.5 7.1 add.109
  732.6 45.2 %reduce-scatter.2.cloned.1.call-done = f32[16,1,64,384]{3,2,0,1:T(8,128)} async-done(((f32[32,1,64,384]{3,2,0,1:T(8,128)}), f32[16,1,64,384]{3,2,0,1:T(8,128)}) %reduce-scatter.2.cloned.1.call-update) | async-done | bytes 1572880 | tf_op jit(solution)/shard_map/reduce_scatter | solution.py:60
  (70 shorter events, 39.7 us)
Async XLA Ops:
  6.5 385.8 %copy-start.1 = (s32[4,8,2]{1,2,0:T(2,128)S(1)}, s32[4,8,2]{1,2,0:T(2,128)}, u32[]{:S(2)}) copy-start(s32[4,8,2]{1,2,0:T(2,128)} %param.10) | copy-start | bytes 772
  6.5 389.8 %copy-start.2 = (s32[256,1,4]{0,2,1:T(4,128)S(1)}, s32[256,1,4]{0,2,1:T(4,128)}, u32[]{:S(2)}) copy-start(s32[256,1,4]{0,2,1:T(4,128)} %param.12) | copy-start | bytes 12292
  6.5 390.1 %copy-start.3 = (s32[32,1,6]{0,1,2:T(1,128)S(1)}, s32[32,1,6]{0,1,2:T(1,128)}, u32[]{:S(2)}) copy-start(s32[32,1,6]{0,1,2:T(1,128)} %param.13) | copy-start | bytes 2308
  6.5 560.8 %all-gather.2.cloned.1.call-start = ((), (), s32[]{:S(2)}) async-start(), calls=%async_computation.3 | async-start | bytes 5242880 | tf_op jit(solution)/shard_map/all_gather | solution.py:41
  6.5 183.6 %collective-permute-start.1 = (f32[256,64,256]{2,1,0:T(8,128)}, f32[256,64,256]{2,1,0:T(8,128)S(1)}, u32[]{:S(2)}, u32[]{:S(2)}) collective-permute-start(f32[256,64,256]{2,1,0:T(8,128)} %bitcast.142), channel_id=1, source_target_pairs={{0,24},{8,0},{16,8},{24,16},{1,25},{9,1},{17,9},{25,17},{2,26},{10... | collective-permute-start | bytes 50331656 | tf_op jit(solution)/shard_map/ppermute | solution.py:9
  190.1 184.7 %copy-start = (f32[256,64,256]{2,1,0:T(8,128)}, f32[256,64,256]{2,1,0:T(8,128)S(1)}, u32[]{:S(2)}) copy-start(f32[256,64,256]{2,1,0:T(8,128)S(1)} %collective-permute-done.1) | copy-start | bytes 50331652
  190.1 182.6 %collective-permute-start.3 = (f32[256,64,256]{2,1,0:T(8,128)S(1)}, f32[256,64,256]{2,1,0:T(8,128)}, u32[]{:S(2)}, u32[]{:S(2)}) collective-permute-start(f32[256,64,256]{2,1,0:T(8,128)S(1)} %collective-permute-done.1), channel_id=1, source_target_pairs={{0,24},{8,0},{16,8},{24,16},{1,25},{9,1},{17,9},{25,17},{2,26},{10... | collective-permute-start | bytes 50331656 | tf_op jit(solution)/shard_map/ppermute | solution.py:9
  372.8 311.4 %collective-permute-start.5 = (f32[256,64,256]{2,1,0:T(8,128)}, f32[256,64,256]{2,1,0:T(8,128)}, u32[]{:S(2)}, u32[]{:S(2)}) collective-permute-start(f32[256,64,256]{2,1,0:T(8,128)} %collective-permute-done.3), channel_id=1, source_target_pairs={{0,24},{8,0},{16,8},{24,16},{1,25},{9,1},{17,9},{25,17},{2,26},{10... | collective-permute-start | bytes 50331656 | tf_op jit(solution)/shard_map/ppermute | solution.py:9
  393.1 7.0 all-to-all-start
  396.3 381.5 %reduce-scatter.2.cloned.1.call-start = ((), (), s32[]{:S(2)}) async-start(), calls=%async_computation.4 | async-start | bytes 4718592 | tf_op jit(solution)/shard_map/reduce_scatter | solution.py:60
  396.5 160.8 %collective-permute-start = (s32[256,4]{1,0:T(8,128)S(1)}, s32[256,4]{1,0:T(8,128)S(1)}, u32[]{:S(2)}, u32[]{:S(2)}) collective-permute-start(s32[256,4]{1,0:T(8,128)S(1)} %bitcast.140), channel_id=1, source_target_pairs={{0,24},{8,0},{16,8},{24,16},{1,25},{9,1},{17,9},{25,17},{2,26},{10... | collective-permute-start | bytes 12296 | tf_op jit(solution)/shard_map/ppermute | solution.py:9
  557.3 4.4 collective-permute-start.2
  561.7 4.9 collective-permute-start.4
Sparse Core Ops, SparseCore 0:
  392.5 81.3 all-gather.1
  732.7 45.0 reduce-scatter.1
where the time goes:
time: 789 us; the launch traced here: 785 us
  waiting for transfers between devices  546 us (69%)
  local copies, waits for them, and re-layouts  95.9 us (12%)
  matrix products  84.5 us (11%)
  blocking collectives  29.8 us (4%)
  starting transfers between devices  13.9 us (2%)
  between operations  13.9 us (2%)
    ppermute x6, waiting for transfers between devices, passed_along(): lax.ppermute(value, axis, [(i, (i + by) % length) for i in range(length)])  498 us
    dot_general x4, matrix products, contribute(): jnp.einsum('rmsbq,rsbk->rmkq', products, matches, precision=lax.Precision...  48.7 us
    reduce_scatter x1, waiting for transfers between devices, on_device(): lax.psum_scatter(partial_sums, 'depth', scatter_dimension=0, tiled=True)  45.2 us
    dot_general x4, matrix products, contribute(): jnp.einsum('rmsj,rsjn->rmsn', a_parts, picked, precision=lax.Precision.HI...  35.9 us
    gather x4, local copies, waits for them, and re-layouts, contribute(): picked = jnp.take(b_vals, a_slots, axis=0)  34.3 us
    reshape x4, local copies, waits for them, and re-layouts, contribute(): products.reshape(rows_here, block_size, slot_count, b_count, block_size)  32.2 us
    all_to_all x1, blocking collectives, on_device(): lax.all_to_all(grouped, 'depth', split_axis=2, concat_axis=0, tiled=True)  16.2 us
  transfers between devices with their start and end apart: 9, of which 7 were waited for; matrix products, arithmetic and copies ran while one was open for 17% of the time, Pallas kernels for 0%

commit v1 on v0

v1 whole, which is shorter than its diff:
```python
import functools

import jax
import jax.numpy as jnp
from jax import lax
from jax.experimental import pallas as pl
from jax.experimental.pallas import tpu as pltpu
from jax.sharding import PartitionSpec as P


def placed_kernel(dims, meta, a_idx, b_idx, m_idx, c_idx, a_end, a_mid, b_own, b_mate, send, keep,
                  a_buf, b_buf, p_buf, a_sem, b_sem):
    x, core, y, piece, take_mid = (meta[n] for n in range(5))
    halves, depths, steps, tiles, slabs, kept, per_row, window, slab = dims
    count = halves * depths * steps

    @pl.when(take_mid == 0)
    def _():
        pltpu.make_async_copy(a_end, a_buf, a_sem).start()

    @pl.when(take_mid != 0)
    def _():
        pltpu.make_async_copy(a_mid, a_buf, a_sem).start()

    my_tile = meta[5]
    rel_tile = jnp.bitwise_xor(my_tile, piece)

    def place(n):
        ex = 1 - n // (depths * steps)
        d = (n // steps) % depths
        t = n % steps
        e = jnp.bitwise_xor(y, d)
        local = piece * depths * steps + d * steps + t
        half = jnp.bitwise_xor(x, ex)
        return ex, e, t, local, half

    def slots_of(n):
        ex, e, t, local, half = place(n)
        base = ((rel_tile * depths + e) * halves + ex) * steps + t
        own_slab = (x * 2 + core) * depths + y
        mate_slab = (x * 2 + 1 - core) * depths + y
        at_own = (base * slabs + own_slab) * per_row
        at_mate = (base * slabs + mate_slab) * per_row
        row = half * 2 + core
        start = jnp.clip(row * (window - 2) - 1, 0, slab - window)
        own = [a_idx[at_own + s] for s in range(per_row)]
        mate = [a_idx[at_mate + s] - start for s in range(per_row)]
        return half, own, mate, start

    def fetch(n, _):
        half, own, mate, _s = slots_of(n)
        for s in range(per_row):
            pltpu.make_async_copy(b_own.at[own[s]], b_buf.at[n, s], b_sem.at[n, s]).start()
            pltpu.make_async_copy(
                b_mate.at[half, mate[s]], b_buf.at[n, per_row + s], b_sem.at[n, per_row + s]
            ).start()
        return 0

    lax.fori_loop(0, count, fetch, 0)
    pltpu.make_async_copy(a_end, a_buf, a_sem).wait()

    size = a_buf.shape[-2]
    wide = 2 * size
    low = lax.broadcasted_iota(jnp.int32, (8, wide), 1) < size

    def work(n, _):
        ex, e, t, local, half = place(n)
        _h, own, mate, start = slots_of(n)
        per_tile = tiles * depths * steps
        c_at = (jnp.where(ex == 0, 0, 1) * per_tile + local) * kept
        c_of = [jnp.where(low, c_idx[c_at + 2 * k], c_idx[c_at + 2 * k + 1]) for k in range(kept // 2)]
        for s in range(2 * per_row):
            pltpu.make_async_copy(b_own.at[0], b_buf.at[n, s], b_sem.at[n, s]).wait()
        for s in range(2 * per_row):
            if s < per_row:
                at = own[s] * 4
                cols = [b_idx[at + b] for b in range(4)]
            else:
                at = (mate[s - per_row] + start) * 4
                cols = [m_idx[at + b] for b in range(4)]
            from0 = jnp.where(low, cols[0], cols[1])
            turn0 = jnp.where(low, cols[1], cols[0])
            from1 = jnp.where(low, cols[2], cols[3])
            turn1 = jnp.where(low, cols[3], cols[2])
            for g in range(size // 8):
                v0 = b_buf[n, s, g * 8:(g + 1) * 8, :wide]
                v1 = b_buf[n, s, g * 8:(g + 1) * 8, wide:]
                r0 = pltpu.roll(v0, size, 1)
                r1 = pltpu.roll(v1, size, 1)
                for k in range(kept // 2):
                    got = (
                        jnp.where(from0 == c_of[k], v0, 0.0)
                        + jnp.where(turn0 == c_of[k], r0, 0.0)
                        + jnp.where(from1 == c_of[k], v1, 0.0)
                        + jnp.where(turn1 == c_of[k], r1, 0.0)
                    )
                    p_buf[s * size + g * 8:s * size + (g + 1) * 8, k * wide:(k + 1) * wide] = got
        a_row = jnp.concatenate(
            [a_buf[ex, e, t, core], a_buf[ex, e, t, 1 - core]], axis=1
        )
        a_hi = a_row.astype(jnp.bfloat16)
        a_lo = (a_row - a_hi.astype(jnp.float32)).astype(jnp.bfloat16)
        p_all = p_buf[...]
        p_hi = p_all.astype(jnp.bfloat16)
        p_lo = (p_all - p_hi.astype(jnp.float32)).astype(jnp.bfloat16)
        both = jnp.dot(jnp.concatenate([a_hi, a_lo], axis=0), p_hi, preferred_element_type=jnp.float32)
        out = both[:size] + (both[size:] + jnp.dot(a_hi, p_lo, preferred_element_type=jnp.float32))

        @pl.when(ex == 1)
        def _():
            send[n] = out

        @pl.when(ex == 0)
        def _():
            keep[n - depths * steps] = out

        return 0

    lax.fori_loop(0, count, work, 0)


def placed_products(dims, meta, a_idx, b_idx, m_idx, c_idx, a_end, a_mid, b_own, b_mate):
    halves, depths, steps, tiles, slabs, kept, per_row, window, slab = dims
    count = halves * depths * steps
    size = a_end.shape[-2]
    shape = jax.ShapeDtypeStruct((depths * steps, size, kept * size), jnp.float32)
    smem = pl.BlockSpec(memory_space=pltpu.SMEM)
    anywhere = pl.BlockSpec(memory_space=pl.ANY)
    vmem = pl.BlockSpec(memory_space=pltpu.VMEM)
    return pl.pallas_call(
        functools.partial(placed_kernel, dims),
        out_shape=(shape, shape),
        in_specs=[smem] * 5 + [anywhere] * 4,
        out_specs=(vmem, vmem),
        scratch_shapes=[
            pltpu.VMEM(a_end.shape, jnp.float32),
            pltpu.VMEM((count, 2 * per_row) + b_own.shape[1:], jnp.float32),
            pltpu.VMEM((2 * per_row * size, kept * size), jnp.float32),
            pltpu.SemaphoreType.DMA,
            pltpu.SemaphoreType.DMA((count, 2 * per_row)),
        ],
        compiler_params=pltpu.CompilerParams(vmem_limit_bytes=24 * 1024 * 1024),
        cost_estimate=pl.CostEstimate(
            flops=count * 6 * size * 2 * per_row * size * kept * size,
            bytes_accessed=count * (2 * per_row * 4 * size * size + kept * size * size + 2 * per_row * size * size) * 4,
            transcendentals=0,
        ),
    )(meta, a_idx, b_idx, m_idx, c_idx, a_end, a_mid, b_own, b_mate)


def on_device(a_blocks, a_index, b_blocks, b_index, c_index):
    rows = lax.axis_size("row")
    tiles = lax.axis_size("col")
    depths = lax.axis_size("depth")
    row = lax.axis_index("row")
    z = lax.axis_index("col")
    y = lax.axis_index("depth")
    x, core = row // 2, row % 2
    halves = rows // 2
    steps, slabs, size, a_width = a_blocks.shape
    per_row = a_index.shape[2]
    kept = c_index.shape[2]
    slab = b_blocks.shape[0]
    window = slab // rows + 2

    mates = [(r, r ^ 1) for r in range(rows)]
    across = [(r, r ^ 2) for r in range(rows)]

    b_own = b_blocks.reshape(slab, size, -1)
    starts = [jnp.clip((h * 2 + 1 - core) * (window - 2) - 1, 0, slab - window) for h in range(halves)]
    b_send = jnp.stack([lax.dynamic_slice_in_dim(b_own, s, window, 0) for s in starts])

    a_by = a_blocks.reshape(steps, halves, 2, depths, size, a_width)

    def a_for(ex, e):
        return lax.dynamic_index_in_dim(
            lax.dynamic_index_in_dim(a_by, x ^ ex, 1, keepdims=False), y ^ e, 2, keepdims=False
        )

    def doubled(value, axis, bit):
        return jnp.concatenate(
            [value, lax.ppermute(value, axis, [(i, i ^ bit) for i in range(lax.axis_size(axis))])]
        )

    first = jnp.concatenate([a_index.reshape(-1), c_index.reshape(-1)])
    pair = doubled(first[None], "row", 2)
    c_pair = pair[:, a_index.size:].reshape(-1)
    a_rel = pair[:, :a_index.size].reshape(-1)
    bit = 1
    while bit < depths:
        a_rel = doubled(a_rel, "depth", bit)
        bit *= 2
    bit = 1
    while bit < tiles:
        a_rel = doubled(a_rel, "col", bit)
        bit *= 2
    b_flat = b_index.reshape(-1)
    m_flat = lax.ppermute(b_flat, "row", mates)

    parts = []
    for ex in range(halves):
        for e in range(depths):
            part = a_for(ex, e)
            if ex or e:
                perm = [
                    (r * depths + d, (r ^ (2 * ex)) * depths + (d ^ e))
                    for r in range(rows)
                    for d in range(depths)
                ]
                part = lax.ppermute(part, ("row", "depth"), perm)
            parts.append(part)
    own = jnp.stack(parts).reshape(halves, depths, steps, 2, size, a_width)
    b_mate = lax.ppermute(b_send, "row", mates)

    near = lax.ppermute(own, "col", [(0, 1), (1, 0), (2, 3), (3, 2)])
    inner = lax.ppermute(own, "col", [(1, 2), (2, 1)])
    outer = lax.ppermute(inner, "col", [(1, 0), (2, 3)])
    through = lax.ppermute(near, "col", [(2, 1), (1, 2)])
    last = lax.ppermute(through, "col", [(1, 0), (2, 3)])

    middle = (z == 1) | (z == 2)
    sources = [(own, own), (near, near), (outer, inner), (last, through)]
    pieces = [z, z ^ 1, jnp.where(z < 2, 2, 1), jnp.where(z < 2, 3, 0)]
    table = [[0, 1, 2, 3], [1, 0, 3, 2], [2, 2, 1, 1], [3, 3, 0, 0]]
    dims = (halves, depths, steps, tiles, slabs, kept, per_row, window, slab)

    sums = []
    for slot in range(tiles):
        meta = jnp.stack([x, core, y, pieces[slot], middle.astype(jnp.int32), z]).astype(jnp.int32)
        send, keep = placed_products(
            dims, meta, a_rel, b_flat, m_flat, c_pair, *sources[slot], b_own, b_mate
        )
        half_sum = keep + lax.ppermute(send, "row", across)
        if depths == 2:
            perm = []
            for c in range(tiles):
                to = table[slot][c] * depths // tiles
                perm.append((c * depths + 1 - to, c * depths + to))
            sums.append(half_sum + lax.ppermute(half_sum, ("col", "depth"), perm))
        else:
            sums.append(lax.psum(half_sum, "depth"))

    if depths == 2:
        mine = (y * tiles // depths) == (z // 2 * 2)
        one = jnp.where(mine, sums[0], sums[2])
        two = jnp.where(mine, sums[1], sums[3])
        one_piece = jnp.where(mine, pieces[0], pieces[2])
        swap = one_piece % 2 == 1
        out = jnp.concatenate([jnp.where(swap, two, one), jnp.where(swap, one, two)])
    else:
        full = jnp.zeros((tiles,) + sums[0].shape, jnp.float32)
        for slot in range(tiles):
            full = lax.dynamic_update_index_in_dim(full, sums[slot], pieces[slot], 0)
        full = full.reshape((-1,) + sums[0].shape[1:])
        share = full.shape[0] // depths
        out = lax.dynamic_slice_in_dim(full, y * share, share, 0)
    return out[:, None]


def solution(mesh):
    return jax.shard_map(
        on_device,
        mesh=mesh,
        in_specs=(
            P(("row", "col", "depth"), None, None, None),
            P(("row", "col", "depth"), None, None),
            P(("row", "depth"), "col", None, None),
            P(("row", "depth"), "col", None),
            P("row", "col", None),
        ),
        out_specs=P(("row", "depth"), "col", None, None),
        check_vma=False,
    )
```

time: 789 us -> 211 us (0.27)
  waiting for transfers between devices: 546 us -> 91.2 us
  local copies, waits for them, and re-layouts: 95.9 us -> 11.2 us
  matrix products: 84.5 us -> 0 us
  Pallas kernels: 0 us -> 44.9 us
  starting transfers between devices: 13.9 us -> 54.8 us
  blocking collectives: 29.8 us -> 0 us
  between operations: 13.9 us -> 0.29 us
    ppermute x6 -> x22, waiting for transfers between devices: 498 us -> 91.2 us  [the longest x4 24.9 us: doubled(): lax.ppermute(value, axis, [(i, i ^ bit) for i in range(lax.axis_size(axis...]
    dot_general x8 -> x0, matrix products: 84.5 us -> none  [the longest x4 48.7 us: contribute(): jnp.einsum('rmsbq,rsbk->rmkq', products, matches, precision=lax.Precision...]
    reshape x11 -> x5, local copies, waits for them, and re-layouts: 45.9 us -> 0.49 us  [the longest x2 0.21 us: on_device(): first = jnp.concatenate([a_index.reshape(-1), c_index.reshape(-1)])]
    reduce_scatter x1 -> x0, waiting for transfers between devices: 45.2 us -> none  [on_device(): lax.psum_scatter(partial_sums, 'depth', scatter_dimension=0, tiled=True)]
    pallas_call x0 -> x4, Pallas kernels: none -> 44.9 us  [placed_products(): pl.pallas_call(functools.partial(placed_kernel, dims), out_shape=(shape,...]
    ppermute x6 -> x22, starting transfers between devices: 10.6 us -> 54.8 us  [the longest x4 25.8 us: doubled(): lax.ppermute(value, axis, [(i, i ^ bit) for i in range(lax.axis_size(axis...]
    gather x8 -> x0, local copies, waits for them, and re-layouts: 36.7 us -> none  [the longest x4 34.3 us: contribute(): picked = jnp.take(b_vals, a_slots, axis=0)]
    all_to_all x1 -> x0, blocking collectives: 16.2 us -> none  [on_device(): lax.all_to_all(grouped, 'depth', split_axis=2, concat_axis=0, tiled=True)]
  transfers between devices with their start and end apart: 9 -> 22, of which waited for: 7 -> 12; matrix products, arithmetic and copies ran while one was open for 17% -> 1% of each run, Pallas kernels for 0% -> 21%
where the time goes in v1:
time: 211 us
  waiting for transfers between devices  91.2 us (43%)
  starting transfers between devices  54.8 us (26%)
  Pallas kernels  44.9 us (21%)
  local copies, waits for them, and re-layouts  11.2 us (5%)
  other arithmetic  8.32 us (4%)
    pallas_call x4, Pallas kernels, placed_products(): pl.pallas_call(functools.partial(placed_kernel, dims), out_shape=(shape,...  44.9 us
    ppermute x4, starting transfers between devices, doubled(): lax.ppermute(value, axis, [(i, i ^ bit) for i in range(lax.axis_size(axis...  25.8 us
    ppermute x4, waiting for transfers between devices, doubled(): lax.ppermute(value, axis, [(i, i ^ bit) for i in range(lax.axis_size(axis...  24.9 us
    ppermute x1, waiting for transfers between devices, on_device(): near = lax.ppermute(own, 'col', [(0, 1), (1, 0), (2, 3), (3, 2)])  21.4 us
    ppermute x4, waiting for transfers between devices, on_device(): half_sum = keep + lax.ppermute(send, 'row', across)  20.2 us
    ppermute x4, starting transfers between devices, on_device(): sums.append(half_sum + lax.ppermute(half_sum, ('col', 'depth'), perm))  13.2 us
    ppermute x4, waiting for transfers between devices, on_device(): sums.append(half_sum + lax.ppermute(half_sum, ('col', 'depth'), perm))  12.4 us
    ppermute x3, waiting for transfers between devices, on_device(): part = lax.ppermute(part, ('row', 'depth'), perm)  12.3 us
  transfers between devices with their start and end apart: 22, of which 12 were waited for; matrix products, arithmetic and copies ran while one was open for 1% of the time, Pallas kernels for 21%

profile of v1, /device:TPU:0, one launch (start us, length us, event | category | flops | bytes accessed | tf_op | source)
XLA Modules:
  0.0 210.7 jit_solution(7116524557226971846)
XLA Ops:
  0.0 4.2 %dynamic-slice_bitcast_fusion.1 = (f32[1,66,64,256]{3,2,1,0:T(8,128)S(1)}, f32[1,66,64,256]{3,2,1,0:T(8,128)S(1)}) fusion(f32[256,1,64,256]{3,2,1,0:T(8,128)} %param.7, s32[]{:T(128)S(6)} %min.7, s32[]{:T(128)S(6)} %min.8), kind=kLoop, calls=%fused_computation.2 | loop fusion | bytes 17301512 | tf_op jit(solution)/shard_map/stack | solution.py:171
  4.2 4.0 %pad_maximum_fusion = f32[2,66,64,256]{3,2,1,0:T(8,128)} fusion(f32[1,66,64,256]{3,2,1,0:T(8,128)S(1)} %get-tuple-element.25, f32[1,66,64,256]{3,2,1,0:T(8,128)S(1)} %get-tuple-element.24), kind=kLoop, calls=%fused_computation | loop fusion | flops 2162688 | bytes 17301504 | tf_op jit(solution)/shard_map/stack | solution.py:171
  8.8 2.6 %collective-permute-start.5 = (f32[4,2,64,128]{3,2,1,0:T(8,128)S(1)}, f32[4,2,64,128]{3,2,1,0:T(8,128)S(1)}, u32[]{:S(2)}, u32[]{:S(2)}) collective-permute-start(f32[4,2,64,128]{3,2,1,0:T(8,128)S(1)} %get-tuple-element.29), channel_id=1, source_target_pairs={{0,1},{1,0},{8,9},{9,8},{16,17},{17,16},{24,25},{25,24},{2,3},{3,2... | collective-permute-start | bytes 786440 | tf_op jit(solution)/shard_map/ppermute | solution.py:210
  12.9 5.4 %collective-permute-done.5 = f32[4,2,64,128]{3,2,1,0:T(8,128)S(1)} collective-permute-done((f32[4,2,64,128]{3,2,1,0:T(8,128)S(1)}, f32[4,2,64,128]{3,2,1,0:T(8,128)S(1)}, u32[]{:S(2)}, u32[]{:S(2)}) %collective-permute-start.5) | collective-permute-done | bytes 262176 | tf_op jit(solution)/shard_map/ppermute | solution.py:210
  18.4 2.2 %collective-permute-done.6 = f32[4,2,64,128]{3,2,1,0:T(8,128)S(1)} collective-permute-done((f32[4,2,64,128]{3,2,1,0:T(8,128)S(1)}, f32[4,2,64,128]{3,2,1,0:T(8,128)S(1)}, u32[]{:S(2)}, u32[]{:S(2)}) %collective-permute-start.6) | collective-permute-done | bytes 262176 | tf_op jit(solution)/shard_map/ppermute | solution.py:210
  20.5 4.7 %collective-permute-done.7 = f32[4,2,64,128]{3,2,1,0:T(8,128)S(1)} collective-permute-done((f32[4,2,64,128]{3,2,1,0:T(8,128)S(1)}, f32[4,2,64,128]{3,2,1,0:T(8,128)S(1)}, u32[]{:S(2)}, u32[]{:S(2)}) %collective-permute-start.7) | collective-permute-done | bytes 262176 | tf_op jit(solution)/shard_map/ppermute | solution.py:210
  25.3 1.8 collective-permute-start.8
  27.1 1.7 collective-permute-start.18
  28.8 21.4 %collective-permute-done.8.a_end.a_mid = f32[2,2,4,2,64,128]{5,4,3,2,1,0:T(8,128)S(1)} collective-permute-done((f32[2,2,4,2,64,128]{5,4,3,2,1,0:T(8,128)S(1)}, f32[2,2,4,2,64,128]{5,4,3,2,1,0:T(8,128)S(1)}, u32[]{:S(2)}, u32[]{:S(2)}) %collective-permute-start.8) | collective-permute-done | bytes 1048608 | tf_op jit(solution)/shard_map/ppermute | solution.py:215
  57.9 2.0 collective-permute-done.1
  59.9 23.1 %collective-permute-start.2 = (s32[256]{0:T(256)S(1)}, s32[256]{0:T(256)S(1)}, u32[]{:S(2)}, u32[]{:S(2)}) collective-permute-start(s32[256]{0:T(256)S(1)} %pad_add_fusion.3), channel_id=1, source_target_pairs={{0,2},{2,0},{4,6},{6,4},{1,3},{3,1},{5,7},{7,5},{8,10},{10,8},{12,... | collective-permute-start | bytes 3080 | tf_op jit(solution)/shard_map/ppermute | solution.py:182
  83.0 18.2 %collective-permute-done.2 = s32[256]{0:T(256)S(1)} collective-permute-done((s32[256]{0:T(256)S(1)}, s32[256]{0:T(256)S(1)}, u32[]{:S(2)}, u32[]{:S(2)}) %collective-permute-start.2) | collective-permute-done | bytes 1056 | tf_op jit(solution)/shard_map/ppermute | solution.py:182
  101.2 4.5 %collective-permute-done.3 = s32[512]{0:T(512)S(1)} collective-permute-done((s32[512]{0:T(512)S(1)}, s32[512]{0:T(512)S(1)}, u32[]{:S(2)}, u32[]{:S(2)}) %collective-permute-start.3) | collective-permute-done | bytes 2080 | tf_op jit(solution)/shard_map/ppermute | solution.py:182
  105.7 5.8 %copy-done = f32[256,1,64,256]{3,2,1,0:T(8,128)S(1)} copy-done((f32[256,1,64,256]{3,2,1,0:T(8,128)S(1)}, f32[256,1,64,256]{3,2,1,0:T(8,128)}, u32[]{:S(2)}) %copy-start) | copy-done | bytes 16777240
  111.5 11.3 %shard_map.57 = (f32[8,64,384]{2,1,0:T(8,128)S(1)}, f32[8,64,384]{2,1,0:T(8,128)S(1)}) custom-call(s32[6]{0:T(128)S(1)} %stack.97.meta, s32[1024]{0:T(1024)S(1)} %constant_dynamic-update-slice_fusion.a_idx, s32[1024]{0:T(1024)S(1)} %reshape.40.b_idx, s32[1024]{0:T(1024)S(1)} %collective-permute-done.4.m_idx, s32[384]{0:T(512)S(1)} %reshape.41.c_idx, ...), custom_call_target="tpu_custom_call" | custom-call | flops 603979776 | bytes 6815744 | tf_op jit(solution)/shard_map/pallas_call | solution.py:130
  124.3 11.2 %shard_map.58 = (f32[8,64,384]{2,1,0:T(8,128)S(1)}, f32[8,64,384]{2,1,0:T(8,128)S(1)}) custom-call(s32[6]{0:T(128)S(1)} %stack.99.meta, s32[1024]{0:T(1024)S(1)} %constant_dynamic-update-slice_fusion.a_idx, s32[1024]{0:T(1024)S(1)} %reshape.40.b_idx, s32[1024]{0:T(1024)S(1)} %collective-permute-done.4.m_idx, s32[384]{0:T(512)S(1)} %reshape.41.c_idx, ...), custom_call_target="tpu_custom_call" | custom-call | flops 603979776 | bytes 6815744 | tf_op jit(solution)/shard_map/pallas_call | solution.py:130
  136.1 11.3 %shard_map.55 = (f32[8,64,384]{2,1,0:T(8,128)S(1)}, f32[8,64,384]{2,1,0:T(8,128)S(1)}) custom-call(s32[6]{0:T(128)S(1)} %stack.86.meta, s32[1024]{0:T(1024)S(1)} %constant_dynamic-update-slice_fusion.a_idx, s32[1024]{0:T(1024)S(1)} %reshape.40.b_idx, s32[1024]{0:T(1024)S(1)} %collective-permute-done.4.m_idx, s32[384]{0:T(512)S(1)} %reshape.41.c_idx, ...), custom_call_target="tpu_custom_call" | custom-call | flops 603979776 | bytes 6815744 | tf_op jit(solution)/shard_map/pallas_call | solution.py:130
  148.9 11.2 %shard_map.56 = (f32[8,64,384]{2,1,0:T(8,128)S(1)}, f32[8,64,384]{2,1,0:T(8,128)S(1)}) custom-call(s32[6]{0:T(128)S(1)} %stack.96.meta, s32[1024]{0:T(1024)S(1)} %constant_dynamic-update-slice_fusion.a_idx, s32[1024]{0:T(1024)S(1)} %reshape.40.b_idx, s32[1024]{0:T(1024)S(1)} %collective-permute-done.4.m_idx, s32[384]{0:T(512)S(1)} %reshape.41.c_idx, ...), custom_call_target="tpu_custom_call" | custom-call | flops 603979776 | bytes 6815744 | tf_op jit(solution)/shard_map/pallas_call | solution.py:130
  162.2 6.3 %collective-permute-start.21 = (f32[8,64,384]{2,1,0:T(8,128)S(1)}, f32[8,64,384]{2,1,0:T(8,128)}, u32[]{:S(2)}, u32[]{:S(2)}) collective-permute-start(f32[8,64,384]{2,1,0:T(8,128)S(1)} %add.92), channel_id=1, source_target_pairs={{0,1},{2,3},{5,4},{7,6},{8,9},{10,11},{13,12},{15,14},{16,17},{18,... | collective-permute-start | bytes 2359304 | tf_op jit(solution)/shard_map/ppermute | solution.py:239
  168.6 8.4 %collective-permute-done.10 = f32[8,64,384]{2,1,0:T(8,128)S(1)} collective-permute-done((f32[8,64,384]{2,1,0:T(8,128)S(1)}, f32[8,64,384]{2,1,0:T(8,128)S(1)}, u32[]{:S(2)}, u32[]{:S(2)}) %collective-permute-start.10) | collective-permute-done | bytes 786464 | tf_op jit(solution)/shard_map/ppermute | solution.py:233
  178.4 11.8 %collective-permute-done.14 = f32[8,64,384]{2,1,0:T(8,128)S(1)} collective-permute-done((f32[8,64,384]{2,1,0:T(8,128)S(1)}, f32[8,64,384]{2,1,0:T(8,128)S(1)}, u32[]{:S(2)}, u32[]{:S(2)}) %collective-permute-start.14) | collective-permute-done | bytes 786464 | tf_op jit(solution)/shard_map/ppermute | solution.py:233
  190.3 4.3 %collective-permute-start.15 = (f32[8,64,384]{2,1,0:T(8,128)S(1)}, f32[8,64,384]{2,1,0:T(8,128)}, u32[]{:S(2)}, u32[]{:S(2)}) collective-permute-start(f32[8,64,384]{2,1,0:T(8,128)S(1)} %add.88), channel_id=1, source_target_pairs={{0,1},{2,3},{5,4},{7,6},{8,9},{10,11},{13,12},{15,14},{16,17},{18,... | collective-permute-start | bytes 2359304 | tf_op jit(solution)/shard_map/ppermute | solution.py:239
  195.3 11.7 %collective-permute-done.15 = f32[8,64,384]{2,1,0:T(8,128)} collective-permute-done((f32[8,64,384]{2,1,0:T(8,128)S(1)}, f32[8,64,384]{2,1,0:T(8,128)}, u32[]{:S(2)}, u32[]{:S(2)}) %collective-permute-start.15) | collective-permute-done | bytes 786464 | tf_op jit(solution)/shard_map/ppermute | solution.py:239
  207.0 2.3 %broadcast_select_fusion.1 = (f32[8,64,384]{2,1,0:T(8,128)S(1)}, f32[8,64,384]{2,1,0:T(8,128)S(1)}, f32[8,64,384]{2,1,0:T(8,128)S(1)}) fusion(pred[]{:T(512)S(6)} %eq.16, f32[8,64,384]{2,1,0:T(8,128)S(1)} %add.88, f32[8,64,384]{2,1,0:T(8,128)} %collective-permute-done.15, f32[8,64,384]{2,1,0:T(8,128)S(1)} %add.86, f32[8,64,384]{2,1,0:T(8,128)} %collective-permute-done.11, ...), kind=kLoop, calls=%fused_computation.8 | loop fusion | flops 1376256 | bytes 8650754 | tf_op jit(solution)/shard_map/jit(_where)/select_n | solution.py:249
  (67 shorter events, 19.1 us)
Async XLA Ops:
  4.2 46.7 %copy-start.4 = (s32[32,1,6]{0,1,2:T(1,128)S(1)}, s32[32,1,6]{0,1,2:T(1,128)}, u32[]{:S(2)}) copy-start(s32[32,1,6]{0,1,2:T(1,128)} %param.9) | copy-start | bytes 2308
  4.2 46.9 %copy-start.2 = (s32[4,8,2]{1,2,0:T(2,128)S(1)}, s32[4,8,2]{1,2,0:T(2,128)}, u32[]{:S(2)}) copy-start(s32[4,8,2]{1,2,0:T(2,128)} %param.6) | copy-start | bytes 772
  8.3 97.4 %collective-permute-start.9 = (f32[2,66,64,256]{3,2,1,0:T(8,128)}, f32[2,66,64,256]{3,2,1,0:T(8,128)}, u32[]{:S(2)}, u32[]{:S(2)}) collective-permute-start(f32[2,66,64,256]{3,2,1,0:T(8,128)} %pad_maximum_fusion), channel_id=1, source_target_pairs={{0,8},{8,0},{16,24},{24,16},{1,9},{9,1},{17,25},{25,17},{2,10},{10... | collective-permute-start | bytes 25952264 | tf_op jit(solution)/shard_map/ppermute | solution.py:213
  8.8 9.6 %collective-permute-start.5 = (f32[4,2,64,128]{3,2,1,0:T(8,128)S(1)}, f32[4,2,64,128]{3,2,1,0:T(8,128)S(1)}, u32[]{:S(2)}, u32[]{:S(2)}) collective-permute-start(f32[4,2,64,128]{3,2,1,0:T(8,128)S(1)} %get-tuple-element.29), channel_id=1, source_target_pairs={{0,1},{1,0},{8,9},{9,8},{16,17},{17,16},{24,25},{25,24},{2,3},{3,2... | collective-permute-start | bytes 786440 | tf_op jit(solution)/shard_map/ppermute | solution.py:210
  11.4 9.1 %collective-permute-start.6 = (f32[4,2,64,128]{3,2,1,0:T(8,128)S(1)}, f32[4,2,64,128]{3,2,1,0:T(8,128)S(1)}, u32[]{:S(2)}, u32[]{:S(2)}) collective-permute-start(f32[4,2,64,128]{3,2,1,0:T(8,128)S(1)} %get-tuple-element.28), channel_id=1, source_target_pairs={{0,16},{1,17},{8,24},{9,25},{16,0},{17,1},{24,8},{25,9},{2,18},{3,... | collective-permute-start | bytes 786440 | tf_op jit(solution)/shard_map/ppermute | solution.py:210
  12.9 12.4 %collective-permute-start.7 = (f32[4,2,64,128]{3,2,1,0:T(8,128)S(1)}, f32[4,2,64,128]{3,2,1,0:T(8,128)S(1)}, u32[]{:S(2)}, u32[]{:S(2)}) collective-permute-start(f32[4,2,64,128]{3,2,1,0:T(8,128)S(1)} %get-tuple-element.27), channel_id=1, source_target_pairs={{0,17},{1,16},{8,25},{9,24},{16,1},{17,0},{24,9},{25,8},{2,19},{3,... | collective-permute-start | bytes 786440 | tf_op jit(solution)/shard_map/ppermute | solution.py:210
  25.3 24.8 %collective-permute-start.8 = (f32[2,2,4,2,64,128]{5,4,3,2,1,0:T(8,128)S(1)}, f32[2,2,4,2,64,128]{5,4,3,2,1,0:T(8,128)S(1)}, u32[]{:S(2)}, u32[]{:S(2)}) collective-permute-start(f32[2,2,4,2,64,128]{5,4,3,2,1,0:T(8,128)S(1)} %bitcast.39), channel_id=1, source_target_pairs={{0,2},{2,0},{4,6},{6,4},{1,3},{3,1},{5,7},{7,5},{8,10},{10,8},{12,... | collective-permute-start | bytes 3145736 | tf_op jit(solution)/shard_map/ppermute | solution.py:215
  27.1 24.2 %collective-permute-start.18 = (f32[2,2,4,2,64,128]{5,4,3,2,1,0:T(8,128)S(1)}, f32[2,2,4,2,64,128]{5,4,3,2,1,0:T(8,128)}, u32[]{:S(2)}, u32[]{:S(2)}) collective-permute-start(f32[2,2,4,2,64,128]{5,4,3,2,1,0:T(8,128)S(1)} %bitcast.40), channel_id=1, source_target_pairs={{2,4},{4,2},{3,5},{5,3},{10,12},{12,10},{11,13},{13,11},{18,20},{2... | collective-permute-start | bytes 3145736 | tf_op jit(solution)/shard_map/ppermute | solution.py:216
  50.2 4.6 %collective-permute-start.12 = (f32[2,2,4,2,64,128]{5,4,3,2,1,0:T(8,128)S(1)}, f32[2,2,4,2,64,128]{5,4,3,2,1,0:T(8,128)S(1)}, u32[]{:S(2)}, u32[]{:S(2)}) collective-permute-start(f32[2,2,4,2,64,128]{5,4,3,2,1,0:T(8,128)S(1)} %collective-permute-done.8.a_end.a_mid), channel_id=1, source_target_pairs={{4,2},{2,4},{5,3},{3,5},{12,10},{10,12},{13,11},{11,13},{20,18},{1... | collective-permute-start | bytes 3145736 | tf_op jit(solution)/shard_map/ppermute | solution.py:218
  51.3 73.0 %collective-permute-start.19 = (f32[2,2,4,2,64,128]{5,4,3,2,1,0:T(8,128)}, f32[2,2,4,2,64,128]{5,4,3,2,1,0:T(8,128)}, u32[]{:S(2)}, u32[]{:S(2)}) collective-permute-start(f32[2,2,4,2,64,128]{5,4,3,2,1,0:T(8,128)} %collective-permute-done.18.a_mid), channel_id=1, source_target_pairs={{2,0},{4,6},{3,1},{5,7},{10,8},{12,14},{11,9},{13,15},{18,16},{20,... | collective-permute-start | bytes 3145736 | tf_op jit(solution)/shard_map/ppermute | solution.py:217
  52.7 3.6 %collective-permute-start = (s32[1,256]{1,0:T(1,128)S(1)}, s32[1,256]{1,0:T(1,128)S(1)}, u32[]{:S(2)}, u32[]{:S(2)}) collective-permute-start(s32[1,256]{1,0:T(1,128)S(1)} %bitcast.47), channel_id=1, source_target_pairs={{0,16},{8,24},{16,0},{24,8},{1,17},{9,25},{17,1},{25,9},{2,18},{10... | collective-permute-start | bytes 3080 | tf_op jit(solution)/shard_map/ppermute | solution.py:182
  54.3 51.4 %collective-permute-start.4 = (s32[1024]{0:T(1024)S(1)}, s32[1024]{0:T(1024)S(1)}, u32[]{:S(2)}, u32[]{:S(2)}) collective-permute-start(s32[1024]{0:T(1024)S(1)} %reshape.40.b_idx), channel_id=1, source_target_pairs={{0,8},{8,0},{16,24},{24,16},{1,9},{9,1},{17,25},{25,17},{2,10},{10... | collective-permute-start | bytes 12296 | tf_op jit(solution)/shard_map/ppermute | solution.py:198
  54.7 94.2 %collective-permute-start.13 = (f32[2,2,4,2,64,128]{5,4,3,2,1,0:T(8,128)S(1)}, f32[2,2,4,2,64,128]{5,4,3,2,1,0:T(8,128)}, u32[]{:S(2)}, u32[]{:S(2)}) collective-permute-start(f32[2,2,4,2,64,128]{5,4,3,2,1,0:T(8,128)S(1)} %collective-permute-done.12.a_mid), channel_id=1, source_target_pairs={{2,0},{4,6},{3,1},{5,7},{10,8},{12,14},{11,9},{13,15},{18,16},{20,... | collective-permute-start | bytes 3145736 | tf_op jit(solution)/shard_map/ppermute | solution.py:219
  56.4 3.5 %collective-permute-start.1 = (s32[128]{0:T(128)S(1)}, s32[128]{0:T(128)S(1)}, u32[]{:S(2)}, u32[]{:S(2)}) collective-permute-start(s32[128]{0:T(128)S(1)} %reshape.39), channel_id=1, source_target_pairs={{0,1},{1,0},{2,3},{3,2},{4,5},{5,4},{6,7},{7,6},{8,9},{9,8},{10,11... | collective-permute-start | bytes 1544 | tf_op jit(solution)/shard_map/ppermute | solution.py:182
  59.9 41.3 %collective-permute-start.2 = (s32[256]{0:T(256)S(1)}, s32[256]{0:T(256)S(1)}, u32[]{:S(2)}, u32[]{:S(2)}) collective-permute-start(s32[256]{0:T(256)S(1)} %pad_add_fusion.3), channel_id=1, source_target_pairs={{0,2},{2,0},{4,6},{6,4},{1,3},{3,1},{5,7},{7,5},{8,10},{10,8},{12,... | collective-permute-start | bytes 3080 | tf_op jit(solution)/shard_map/ppermute | solution.py:182
  101.2 4.5 %collective-permute-start.3 = (s32[512]{0:T(512)S(1)}, s32[512]{0:T(512)S(1)}, u32[]{:S(2)}, u32[]{:S(2)}) collective-permute-start(s32[512]{0:T(512)S(1)} %pad_add_fusion.1), channel_id=1, source_target_pairs={{0,4},{2,6},{4,0},{6,2},{1,5},{3,7},{5,1},{7,3},{8,12},{10,14},{12... | collective-permute-start | bytes 6152 | tf_op jit(solution)/shard_map/ppermute | solution.py:182
  122.7 38.0 %collective-permute-start.16 = (f32[8,64,384]{2,1,0:T(8,128)S(1)}, f32[8,64,384]{2,1,0:T(8,128)S(1)}, u32[]{:S(2)}, u32[]{:S(2)}) collective-permute-start(f32[8,64,384]{2,1,0:T(8,128)S(1)} %get-tuple-element.18), channel_id=1, source_target_pairs={{0,16},{8,24},{16,0},{24,8},{1,17},{9,25},{17,1},{25,9},{2,18},{10... | collective-permute-start | bytes 2359304 | tf_op jit(solution)/shard_map/ppermute | solution.py:233
  135.5 26.6 %collective-permute-start.20 = (f32[8,64,384]{2,1,0:T(8,128)S(1)}, f32[8,64,384]{2,1,0:T(8,128)S(1)}, u32[]{:S(2)}, u32[]{:S(2)}) collective-permute-start(f32[8,64,384]{2,1,0:T(8,128)S(1)} %get-tuple-element.20), channel_id=1, source_target_pairs={{0,16},{8,24},{16,0},{24,8},{1,17},{9,25},{17,1},{25,9},{2,18},{10... | collective-permute-start | bytes 2359304 | tf_op jit(solution)/shard_map/ppermute | solution.py:233
  147.4 29.6 %collective-permute-start.10 = (f32[8,64,384]{2,1,0:T(8,128)S(1)}, f32[8,64,384]{2,1,0:T(8,128)S(1)}, u32[]{:S(2)}, u32[]{:S(2)}) collective-permute-start(f32[8,64,384]{2,1,0:T(8,128)S(1)} %get-tuple-element.14), channel_id=1, source_target_pairs={{0,16},{8,24},{16,0},{24,8},{1,17},{9,25},{17,1},{25,9},{2,18},{10... | collective-permute-start | bytes 2359304 | tf_op jit(solution)/shard_map/ppermute | solution.py:233
  160.1 30.0 %collective-permute-start.14 = (f32[8,64,384]{2,1,0:T(8,128)S(1)}, f32[8,64,384]{2,1,0:T(8,128)S(1)}, u32[]{:S(2)}, u32[]{:S(2)}) collective-permute-start(f32[8,64,384]{2,1,0:T(8,128)S(1)} %get-tuple-element.16), channel_id=1, source_target_pairs={{0,16},{8,24},{16,0},{24,8},{1,17},{9,25},{17,1},{25,9},{2,18},{10... | collective-permute-start | bytes 2359304 | tf_op jit(solution)/shard_map/ppermute | solution.py:233
  160.8 33.8 %collective-permute-start.17 = (f32[8,64,384]{2,1,0:T(8,128)S(1)}, f32[8,64,384]{2,1,0:T(8,128)}, u32[]{:S(2)}, u32[]{:S(2)}) collective-permute-start(f32[8,64,384]{2,1,0:T(8,128)S(1)} %add.90), channel_id=1, source_target_pairs={{1,0},{3,2},{4,5},{6,7},{9,8},{11,10},{12,13},{14,15},{17,16},{19,... | collective-permute-start | bytes 2359304 | tf_op jit(solution)/shard_map/ppermute | solution.py:239
  162.2 32.4 %collective-permute-start.21 = (f32[8,64,384]{2,1,0:T(8,128)S(1)}, f32[8,64,384]{2,1,0:T(8,128)}, u32[]{:S(2)}, u32[]{:S(2)}) collective-permute-start(f32[8,64,384]{2,1,0:T(8,128)S(1)} %add.92), channel_id=1, source_target_pairs={{0,1},{2,3},{5,4},{7,6},{8,9},{10,11},{13,12},{15,14},{16,17},{18,... | collective-permute-start | bytes 2359304 | tf_op jit(solution)/shard_map/ppermute | solution.py:239
  177.1 18.2 %collective-permute-start.11 = (f32[8,64,384]{2,1,0:T(8,128)S(1)}, f32[8,64,384]{2,1,0:T(8,128)}, u32[]{:S(2)}, u32[]{:S(2)}) collective-permute-start(f32[8,64,384]{2,1,0:T(8,128)S(1)} %add.86), channel_id=1, source_target_pairs={{1,0},{3,2},{4,5},{6,7},{9,8},{11,10},{12,13},{14,15},{17,16},{19,... | collective-permute-start | bytes 2359304 | tf_op jit(solution)/shard_map/ppermute | solution.py:239
  190.3 16.8 %collective-permute-start.15 = (f32[8,64,384]{2,1,0:T(8,128)S(1)}, f32[8,64,384]{2,1,0:T(8,128)}, u32[]{:S(2)}, u32[]{:S(2)}) collective-permute-start(f32[8,64,384]{2,1,0:T(8,128)S(1)} %add.88), channel_id=1, source_target_pairs={{0,1},{2,3},{5,4},{7,6},{8,9},{10,11},{13,12},{15,14},{16,17},{18,... | collective-permute-start | bytes 2359304 | tf_op jit(solution)/shard_map/ppermute | solution.py:239
  (3 other events, 56.1 us)

commit v2 on v0

v2 whole, which is shorter than its diff:
```python
import functools

import jax
import jax.numpy as jnp
from jax import lax
from jax.experimental import pallas as pl
from jax.experimental.pallas import tpu as pltpu
from jax.sharding import PartitionSpec as P

LANES = 128
INDEX_ROWS = 8
COST = 1000000000
VMEM_BYTES = 48 * 1024 * 1024
CUTS = (1, 1, 2, 2)
Y_WITH = {0: 1, 1: 3, 2: 4, 3: 5, 4: 5, 5: 5}
SETTLE = {6: [0, 1, 2, 3, 4, 5]}


def slot_piece(slot, z, tiles):
    if slot == 0:
        return z
    if slot == 1:
        return jnp.bitwise_xor(z, 1)
    if slot == 2:
        return jnp.where(z < tiles // 2, 2, 1)
    return jnp.where(z < tiles // 2, 3, 0)


def placed_kernel(dims, slot, first, count, across, table, a_refs, b_own, b_mate, after, send, keep,
                  a_buf, i_wide, i_whole, i_buf, b_buf, p_hi, p_lo, a_sem, i_sem, b_sem):
    halves, depths, steps, tiles, kept, per_row, b_count, slab, size, near_rows = dims
    x, core, y, z = (table[n] for n in range(4))
    at_mine, at_mate = 8, 8 + slab * b_count
    at_kept = at_mate + slab * b_count
    data_rows = steps * 2 * size
    part_rows = data_rows + INDEX_ROWS
    wide = 2 * size
    per_piece = depths * steps
    per_tile = tiles * per_piece
    piece = slot_piece(slot, z, tiles)
    middle = jnp.logical_and(z > 0, z < tiles - 1)

    def loads(refs):
        index, copies = [], []
        which = 0
        for ref in refs:
            for part in range(ref.shape[0] // part_rows):
                index.append(
                    pltpu.make_async_copy(
                        ref.at[pl.ds(part * part_rows + data_rows, INDEX_ROWS)],
                        i_wide.at[pl.ds(which * INDEX_ROWS, INDEX_ROWS)],
                        i_sem.at[which],
                    )
                )
                copies.append(
                    pltpu.make_async_copy(
                        ref.at[pl.ds(part * part_rows, data_rows)],
                        a_buf.at[pl.ds(which * data_rows, data_rows)],
                        a_sem.at[which],
                    )
                )
                which += 1
        return index + copies

    starts, rows = [], []
    for ex in range(halves):
        block_row = (jnp.bitwise_xor(x, ex) * 2 + core) * per_tile + piece * per_piece + first
        start = jnp.clip(block_row * slab // (halves * 2 * per_tile) - 1, 0, slab - near_rows)
        band = pl.ds(pl.multiple_of(start * size, size), near_rows * size)
        rows.append(
            [
                pltpu.make_async_copy(source.at[band], b_buf.at[ex, number], b_sem.at[ex, number])
                for number, source in enumerate((b_own, b_mate))
            ]
        )
        starts.append(start)
    for ex in reversed(range(halves)):
        for copy in rows[ex]:
            copy.start()
    if len(a_refs) == 1:
        data = loads(a_refs[0])
        for copy in data:
            copy.start()
    else:
        @pl.when(middle)
        def _():
            for copy in loads(a_refs[1]):
                copy.start()

        @pl.when(jnp.logical_not(middle))
        def _():
            for copy in loads(a_refs[0]):
                copy.start()

        data = loads(a_refs[0])
    for copy in data[:halves * across]:
        copy.wait()
    data = data[halves * across:]
    i_whole[...] = i_wide[...].astype(jnp.int32)
    whole = pltpu.make_async_copy(i_whole, i_buf, i_sem.at[halves * across])
    whole.start()
    whole.wait()

    low = lax.broadcasted_iota(jnp.int32, (8, wide), 1) < size

    def place(n):
        d = (first + n) // steps
        return jnp.bitwise_xor(y, d) % across, (first + n) % steps

    def build(ex, n, high, low_part):
        e, t = place(n)
        c_at = at_kept + (ex * per_tile + piece * per_piece + first + n) * kept
        c_of = [jnp.where(low, table[c_at + 2 * k], table[c_at + 2 * k + 1]) for k in range(kept // 2)]
        for s in range(2 * per_row):
            whose = core if s < per_row else 1 - core
            row = i_buf[(ex * across + e) * INDEX_ROWS, (t * 2 + whose) * per_row + s % per_row]
            at = (at_mine if s < per_row else at_mate) + row * b_count
            cols = [table[at + b] for b in range(b_count)]
            held_at = pl.multiple_of((row - starts[ex]) * size, size)
            wanted = []
            for b in range(0, b_count, 2):
                wanted.append(jnp.where(low, cols[b], cols[b + 1]))
                wanted.append(jnp.where(low, cols[b + 1], cols[b]))
            held = []
            for g in range(size // 8):
                row = []
                for b in range(b_count // 2):
                    v = b_buf[ex, s // per_row, pl.ds(held_at + g * 8, 8), b * wide:(b + 1) * wide]
                    row += [v, pltpu.roll(v, size, 1)]
                held.append(row)
            for k in range(kept // 2):
                masks = [w == c_of[k] for w in wanted]
                for pair in range(size // 16):
                    both = []
                    for g in (2 * pair, 2 * pair + 1):
                        got = jnp.where(masks[0], held[g][0], 0.0)
                        for m in range(1, b_count):
                            got = got + jnp.where(masks[m], held[g][m], 0.0)
                        both.append(got)
                    both = jnp.concatenate(both, axis=0)
                    hi = both.astype(jnp.bfloat16)
                    lo = (both - hi.astype(jnp.float32)).astype(jnp.bfloat16)
                    rows = slice(s * size + pair * 16, s * size + (pair + 1) * 16)
                    high[rows, k * wide:(k + 1) * wide] = hi
                    low_part[rows, k * wide:(k + 1) * wide] = lo

    def multiply(ex, n, high, low_part):
        e, t = place(n)
        base = (ex * across + e) * data_rows + t * 2 * size
        a_row = jnp.concatenate(
            [
                a_buf[pl.ds(pl.multiple_of(base + core * size, size), size)],
                a_buf[pl.ds(pl.multiple_of(base + (1 - core) * size, size), size)],
            ],
            axis=1,
        )
        a_hi = a_row.astype(jnp.bfloat16)
        a_lo = (a_row - a_hi.astype(jnp.float32)).astype(jnp.bfloat16)
        both = jnp.dot(jnp.concatenate([a_hi, a_lo], axis=0), high[...], preferred_element_type=jnp.float32)
        return both[:size] + (both[size:] + jnp.dot(a_hi, low_part[...], preferred_element_type=jnp.float32))

    for ex in reversed(range(halves)):
        for copy in rows[ex]:
            copy.wait()
        if ex == halves - 1:
            for copy in data:
                copy.wait()

        def two(m, _, ex=ex):
            for u in range(2):
                build(ex, 2 * m + u, p_hi[u], p_lo[u])
            for u in range(2):
                out = multiply(ex, 2 * m + u, p_hi[u], p_lo[u])
                if ex:
                    send[2 * m + u] = out
                else:
                    keep[2 * m + u] = out
            return 0

        lax.fori_loop(0, count // 2, two, 0)


def placed_products(dims, slot, first, count, across, table, a_sources, b_own, b_mate, after):
    halves, depths, steps, tiles, kept, per_row, b_count, slab, size, near_rows = dims
    shape = jax.ShapeDtypeStruct((count, size, kept * size), jnp.float32)
    smem = pl.BlockSpec(memory_space=pltpu.SMEM)
    anywhere = pl.BlockSpec(memory_space=pl.ANY)
    hbm = pl.BlockSpec(memory_space=pltpu.HBM)
    vmem = pl.BlockSpec(memory_space=pltpu.VMEM)
    parts = halves * across
    placed_shape = pltpu.VMEM((2 * per_row * size, kept * size), jnp.bfloat16)
    return pl.pallas_call(
        functools.partial(placed_kernel, dims, slot, first, count, across),
        out_shape=(shape, shape),
        in_specs=[smem] + [jax.tree.map(lambda _: anywhere, a_sources), hbm, hbm, [anywhere] * len(after)],
        out_specs=(vmem, vmem),
        scratch_shapes=[
            pltpu.VMEM((parts * steps * 2 * size, LANES), jnp.float32),
            pltpu.VMEM((parts * INDEX_ROWS, LANES), jnp.float32),
            pltpu.VMEM((parts * INDEX_ROWS, LANES), jnp.int32),
            pltpu.SMEM((parts * INDEX_ROWS, LANES), jnp.int32),
            pltpu.VMEM((halves, 2, near_rows * size, b_own.shape[1]), jnp.float32),
            [placed_shape] * 2,
            [placed_shape] * 2,
            pltpu.SemaphoreType.DMA((parts,)),
            pltpu.SemaphoreType.DMA((parts + 1,)),
            pltpu.SemaphoreType.DMA((halves, 2)),
        ],
        compiler_params=pltpu.CompilerParams(vmem_limit_bytes=VMEM_BYTES),
        cost_estimate=pl.CostEstimate(
            flops=COST * count * halves,
            bytes_accessed=4 * (2 * count * size * kept * size + parts * steps * 2 * size * LANES),
            transcendentals=0,
        ),
    )(table, a_sources, b_own, b_mate, after)


def joined_kernel(parts, after, out, sem):
    copies = []
    at = 0
    for number, part in enumerate(parts):
        copies.append(pltpu.make_async_copy(part, out.at[pl.ds(at, part.shape[0])], sem.at[number]))
        at += part.shape[0]
    for copy in copies:
        copy.start()
    for copy in copies:
        copy.wait()


def joined(parts, after):
    anywhere = pl.BlockSpec(memory_space=pl.ANY)
    total = sum(part.shape[0] for part in parts)
    return pl.pallas_call(
        joined_kernel,
        out_shape=jax.ShapeDtypeStruct((total,) + parts[0].shape[1:], jnp.float32),
        in_specs=[[anywhere] * len(parts), [anywhere] * len(after)],
        out_specs=pl.BlockSpec(memory_space=pltpu.VMEM),
        scratch_shapes=[pltpu.SemaphoreType.DMA((len(parts),))],
        compiler_params=pltpu.CompilerParams(vmem_limit_bytes=VMEM_BYTES),
        cost_estimate=pl.CostEstimate(flops=0, bytes_accessed=8 * total * LANES, transcendentals=0),
    )(parts, after)


def settle_kernel(slot, first, depths, steps, tiles, table, total, other, *refs):
    out, held, sem = refs[-3:]
    y, z = table[2], table[3]
    piece = slot_piece(slot, z, tiles)

    @pl.when(piece * depths // tiles == y)
    def _():
        held[...] = total[...] + other[...]
        at = piece % (tiles // depths) * depths * steps + first
        copy = pltpu.make_async_copy(held, out.at[pl.ds(at, total.shape[0]), 0], sem)
        copy.start()
        copy.wait()


def settled(slot, first, depths, steps, tiles, meta, total, other, out):
    anywhere = pl.BlockSpec(memory_space=pl.ANY)
    vmem = pl.BlockSpec(memory_space=pltpu.VMEM)
    shape = jax.ShapeDtypeStruct((tiles * steps, 1) + total.shape[1:], jnp.float32)
    so_far = [] if out is None else [out]
    return pl.pallas_call(
        functools.partial(settle_kernel, slot, first, depths, steps, tiles),
        out_shape=shape,
        in_specs=[pl.BlockSpec(memory_space=pltpu.SMEM), vmem, vmem] + [anywhere] * len(so_far),
        out_specs=anywhere,
        scratch_shapes=[pltpu.VMEM(total.shape, jnp.float32), pltpu.SemaphoreType.DMA],
        input_output_aliases={3: 0} if so_far else {},
        compiler_params=pltpu.CompilerParams(vmem_limit_bytes=VMEM_BYTES),
        cost_estimate=pl.CostEstimate(flops=0, bytes_accessed=12 * total.size, transcendentals=0),
    )(meta, total, other, *so_far)


def gate_kernel(value, after, out):
    pass


def gated(value, after):
    anywhere = pl.BlockSpec(memory_space=pl.ANY)
    return pl.pallas_call(
        gate_kernel,
        out_shape=jax.ShapeDtypeStruct(value.shape, value.dtype),
        in_specs=[anywhere, [anywhere] * len(after)],
        out_specs=anywhere,
        input_output_aliases={0: 0},
        cost_estimate=pl.CostEstimate(flops=0, bytes_accessed=0, transcendentals=0),
    )(value, after)


def sum_kernel(one, two, after, out):
    out[...] = one[...] + two[...]


def summed(one, two, after):
    vmem = pl.BlockSpec(memory_space=pltpu.VMEM)
    return pl.pallas_call(
        sum_kernel,
        out_shape=jax.ShapeDtypeStruct(one.shape, one.dtype),
        in_specs=[vmem, vmem, [pl.BlockSpec(memory_space=pl.ANY)] * len(after)],
        out_specs=vmem,
        compiler_params=pltpu.CompilerParams(vmem_limit_bytes=VMEM_BYTES),
        cost_estimate=pl.CostEstimate(flops=one.size, bytes_accessed=12 * one.size, transcendentals=0),
    )(one, two, after)


def split_kernel(halves, depths, cuts, meta, value, after, *refs):
    outs, sem = refs[:cuts], refs[cuts]
    y = meta[2]
    across = depths // cuts
    length = value.shape[0] // (halves * cuts)
    copies = []
    for ex in range(halves):
        for cut in range(cuts):
            at = pl.multiple_of((ex * cuts + jnp.bitwise_xor(y // across, cut)) * length, 8)
            copies.append(
                pltpu.make_async_copy(
                    value.at[pl.ds(at, length)], outs[cut].at[pl.ds(ex * length, length)], sem.at[ex, cut]
                )
            )
    for copy in copies:
        copy.start()
    for copy in copies:
        copy.wait()


def split(halves, depths, cuts, meta, value, after):
    anywhere = pl.BlockSpec(memory_space=pl.ANY)
    shape = jax.ShapeDtypeStruct((value.shape[0] // cuts, value.shape[1]), value.dtype)
    return pl.pallas_call(
        functools.partial(split_kernel, halves, depths, cuts),
        out_shape=(shape,) * cuts,
        in_specs=[pl.BlockSpec(memory_space=pltpu.SMEM), anywhere, [anywhere] * len(after)],
        out_specs=(pl.BlockSpec(memory_space=pltpu.VMEM),) * cuts,
        scratch_shapes=[pltpu.SemaphoreType.DMA((halves, cuts))],
        compiler_params=pltpu.CompilerParams(vmem_limit_bytes=VMEM_BYTES),
        cost_estimate=pl.CostEstimate(flops=0, bytes_accessed=8 * value.size, transcendentals=0),
    )(meta, value, after)


def along(value, step):
    pairs = {
        "near": [(0, 1), (1, 0), (2, 3), (3, 2)],
        "inner": [(1, 2), (2, 1)],
        "outer": [(1, 0), (2, 3)],
        "through": [(2, 1), (1, 2)],
        "last": [(1, 0), (2, 3)],
    }
    with jax.named_scope(step):
        return lax.ppermute(value, "col", pairs[step])


def on_device(a_blocks, a_index, b_blocks, b_index, c_index):
    rows = lax.axis_size("row")
    tiles = lax.axis_size("col")
    depths = lax.axis_size("depth")
    row = lax.axis_index("row")
    z = lax.axis_index("col")
    y = lax.axis_index("depth")
    x, core = row // 2, row % 2
    halves = rows // 2
    steps, slabs, size, a_width = a_blocks.shape
    per_row = a_index.shape[2]
    b_count = b_index.shape[2]
    kept = c_index.shape[2]
    slab = b_blocks.shape[0]
    meta = jnp.stack([x, core, y, z]).astype(jnp.int32)

    mates = [(r, r ^ 1) for r in range(rows)]
    across = [(r, r ^ 2) for r in range(rows)]

    b_own = b_blocks.reshape(slab * size, -1)
    b_flat = b_index.reshape(-1)
    with jax.named_scope("mate"):
        b_mate = lax.ppermute(b_own, "row", mates)
    with jax.named_scope("mate_index"):
        m_flat = lax.ppermute(b_flat, "row", mates)

    a_by = a_blocks.reshape(steps, halves, 2, depths, size, a_width)
    i_by = a_index.reshape(steps, halves, 2, depths, per_row).astype(jnp.float32)
    c_rows = c_index.reshape(-1).astype(jnp.float32)
    c_rows = jnp.pad(c_rows, (0, (INDEX_ROWS - 1) * LANES - c_rows.size)).reshape(-1, LANES)

    def a_for(ex, e):
        def pick(value):
            value = lax.dynamic_index_in_dim(value, x ^ ex, 1, keepdims=False)
            return lax.dynamic_index_in_dim(value, y ^ e, 2, keepdims=False)

        index = pick(i_by).reshape(1, -1)
        index = jnp.pad(index, ((0, 0), (0, LANES - index.shape[1])))
        return jnp.concatenate([pick(a_by).reshape(-1, LANES), index, c_rows])

    own = a_for(0, 0)
    others = [own]
    for ex in range(halves):
        for e in range(depths):
            if ex or e:
                perm = [
                    (r * depths + d, (r ^ (2 * ex)) * depths + (d ^ e))
                    for r in range(rows)
                    for d in range(depths)
                ]
                with jax.named_scope(f"spread_{ex}{e}"):
                    others.append(lax.ppermute(a_for(ex, e), ("row", "depth"), perm))
    c_across = others[depths][1 - INDEX_ROWS:].reshape(-1)[:c_index.size].astype(jnp.int32)
    with jax.named_scope("joined"):
        here = joined(others, [])
    near, inner = along(here, "near"), along(here, "inner")
    whole_table = jnp.concatenate(
        [jnp.pad(meta, (0, 4)), b_flat, m_flat, c_index.reshape(-1), c_across]
    )

    table = [[0, 1, 2, 3], [1, 0, 3, 2], [2, 2, 1, 1], [3, 3, 0, 0]]
    per_piece = depths * steps
    part_rows = own.shape[0]
    data_rows = part_rows - INDEX_ROWS
    block_rows = rows * tiles * per_piece

    x_sums, settle, pending, order = [], [], [], []
    out = None
    number = 0
    for slot in range(tiles):
        if slot == 0:
            a_sources = [[[here]]]
        elif slot == 1:
            near = gated(near, order)
            outer, through = along(inner, "outer"), along(near, "through")
            a_sources = [[[near]]]
        elif slot == 2:
            a_sources = [[[outer], [inner]]]
            throughs = split(halves, depths, CUTS[3], meta, through, order + [outer])
            lasts = [along(value, "last") for value in throughs]
        else:
            a_sources = [[[there], [here]] for there, here in zip(lasts, throughs)]
        cuts = CUTS[slot]
        count = per_piece // cuts
        near_rows = -(-count * slab // block_rows) + 2
        dims = (halves, depths, steps, tiles, kept, per_row, b_count, slab, size, near_rows)
        for cut in range(cuts):
            after = list(order)
            if depths == 2:
                for n in SETTLE.get(number, []):
                    out = settled(*settle[n], out)
                    after.append(out)
            across_here = depths if len(a_sources) == 1 else depths // cuts
            with jax.named_scope(f"placed_{slot}{cut}"):
                send, keep = placed_products(
                    dims, slot, cut * count, count, across_here, whole_table, a_sources[cut % len(a_sources)], b_own, b_mate, after
                )
            order = [keep]
            with jax.named_scope(f"x_{slot}{cut}"):
                other = lax.ppermute(send, "row", across)
            x_sums.append((keep, other))
            if depths == 2:
                perm = []
                for c in range(tiles):
                    to = table[slot][c] * depths // tiles
                    perm.append((c * depths + 1 - to, c * depths + to))
                settle.append(None)
                pending.append((number, slot, cut, count, perm))
                for item in [p for p in pending if Y_WITH[p[0]] <= number]:
                    pending.remove(item)
                    n, its_slot, its_cut, its_count, its_perm = item
                    with jax.named_scope(f"sum_{its_slot}{its_cut}"):
                        total = summed(*x_sums[n], order)
                    with jax.named_scope(f"y_{its_slot}{its_cut}"):
                        other = lax.ppermute(total, ("col", "depth"), its_perm)
                    settle[n] = (its_slot, its_cut * its_count, depths, steps, tiles, meta, total, other)
            number += 1

    if depths == 2:
        for n in SETTLE[number]:
            out = settled(*settle[n], out)
    if depths != 2:
        full = jnp.zeros((tiles, per_piece) + x_sums[0][0].shape[1:], jnp.float32)
        at = 0
        for slot in range(tiles):
            total = lax.psum(jnp.concatenate([one + two for one, two in x_sums[at:at + CUTS[slot]]]), "depth")
            at += CUTS[slot]
            full = lax.dynamic_update_index_in_dim(full, total, slot_piece(slot, z, tiles), 0)
        full = full.reshape((tiles * per_piece,) + x_sums[0][0].shape[1:])
        share = full.shape[0] // depths
        out = lax.dynamic_slice_in_dim(full, y * share, share, 0)[:, None]
    return out


def solution(mesh):
    return jax.shard_map(
        on_device,
        mesh=mesh,
        in_specs=(
            P(("row", "col", "depth"), None, None, None),
            P(("row", "col", "depth"), None, None),
            P(("row", "depth"), "col", None, None),
            P(("row", "depth"), "col", None),
            P("row", "col", None),
        ),
        out_specs=P(("row", "depth"), "col", None, None),
        check_vma=False,
    )
```

time: 789 us -> 158 us (0.20)
  waiting for transfers between devices: 546 us -> 71 us
  local copies, waits for them, and re-layouts: 95.9 us -> 4.93 us
  matrix products: 84.5 us -> 0 us
  Pallas kernels: 0 us -> 46.6 us
  blocking collectives: 29.8 us -> 0 us
  starting transfers between devices: 13.9 us -> 33.9 us
  between operations: 13.9 us -> 0.4 us
    ppermute x6 -> x23, waiting for transfers between devices: 498 us -> 71 us  [the longest x6 40.3 us: along(): return lax.ppermute(value, 'col', pairs[step])]
    dot_general x8 -> x0, matrix products: 84.5 us -> none  [the longest x4 48.7 us: contribute(): jnp.einsum('rmsbq,rsbk->rmkq', products, matches, precision=lax.Precision...]
    pallas_call x0 -> x21, Pallas kernels: none -> 46.6 us  [the longest x6 38 us: placed_products(): pl.pallas_call(functools.partial(placed_kernel, dims, slot, first, count,...]
    reshape x11 -> x8, local copies, waits for them, and re-layouts: 45.9 us -> 0.57 us  [the longest x4 0.35 us: a_for(): index = pick(i_by).reshape(1, -1)]
    reduce_scatter x1 -> x0, waiting for transfers between devices: 45.2 us -> none  [on_device(): lax.psum_scatter(partial_sums, 'depth', scatter_dimension=0, tiled=True)]
    gather x8 -> x0, local copies, waits for them, and re-layouts: 36.7 us -> none  [the longest x4 34.3 us: contribute(): picked = jnp.take(b_vals, a_slots, axis=0)]
    ppermute x6 -> x23, starting transfers between devices: 10.6 us -> 33.9 us  [the longest x6 12.3 us: on_device(): other = lax.ppermute(total, ('col', 'depth'), its_perm)]
    all_to_all x1 -> x0, blocking collectives: 16.2 us -> none  [on_device(): lax.all_to_all(grouped, 'depth', split_axis=2, concat_axis=0, tiled=True)]
  transfers between devices with their start and end apart: 9 -> 23, of which waited for: 7 -> 12; matrix products, arithmetic and copies ran while one was open for 17% -> 3% of each run, Pallas kernels for 0% -> 29%
where the time goes in v2:
time: 158 us; the launch traced here: 157 us
  waiting for transfers between devices  71 us (45%)
  Pallas kernels  46.6 us (29%)
  starting transfers between devices  33.9 us (21%)
  local copies, waits for them, and re-layouts  4.93 us (3%)
    ppermute x6, waiting for transfers between devices, along(): return lax.ppermute(value, 'col', pairs[step])  40.3 us
    pallas_call x6, Pallas kernels, placed_products(): pl.pallas_call(functools.partial(placed_kernel, dims, slot, first, count,...  38 us
    ppermute x6, waiting for transfers between devices, on_device(): other = lax.ppermute(total, ('col', 'depth'), its_perm)  14.4 us
    ppermute x3, waiting for transfers between devices, on_device(): others.append(lax.ppermute(a_for(ex, e), ('row', 'depth'), perm))  12.4 us
    ppermute x6, starting transfers between devices, on_device(): other = lax.ppermute(total, ('col', 'depth'), its_perm)  12.3 us
    ppermute x6, starting transfers between devices, along(): return lax.ppermute(value, 'col', pairs[step])  9.65 us
    ppermute x6, starting transfers between devices, on_device(): other = lax.ppermute(send, 'row', across)  7.23 us
    pallas_call x6, Pallas kernels, settled(): pl.pallas_call(functools.partial(settle_kernel, slot, first, depths, step...  5.29 us
  transfers between devices with their start and end apart: 23, of which 12 were waited for; matrix products, arithmetic and copies ran while one was open for 3% of the time, Pallas kernels for 29%

profile of v2, /device:TPU:0, one launch (start us, length us, event | category | flops | bytes accessed | tf_op | source)
XLA Modules:
  0.0 157.0 jit_solution(4516341564677284900)
XLA Ops:
  4.3 3.5 %collective-permute-start.3 = (f32[520,128]{1,0:T(8,128)S(1)}, f32[520,128]{1,0:T(8,128)S(1)}, u32[]{:S(2)}, u32[]{:S(2)}) collective-permute-start(f32[520,128]{1,0:T(8,128)S(1)} %get-tuple-element.41), channel_id=1, source_target_pairs={{0,17},{1,16},{8,25},{9,24},{16,1},{17,0},{24,9},{25,8},{2,19},{3,... | collective-permute-start | bytes 798728 | tf_op jit(solution)/shard_map/spread_11/ppermute | solution.py:404
  8.5 6.6 %collective-permute-done.3.parts_3_ = f32[520,128]{1,0:T(8,128)S(1)} collective-permute-done((f32[520,128]{1,0:T(8,128)S(1)}, f32[520,128]{1,0:T(8,128)S(1)}, u32[]{:S(2)}, u32[]{:S(2)}) %collective-permute-start.3) | collective-permute-done | bytes 266272 | tf_op jit(solution)/shard_map/spread_11/ppermute | solution.py:404
  15.1 5.5 %collective-permute-done.2.parts_1_ = f32[520,128]{1,0:T(8,128)S(1)} collective-permute-done((f32[520,128]{1,0:T(8,128)S(1)}, f32[520,128]{1,0:T(8,128)S(1)}, u32[]{:S(2)}, u32[]{:S(2)}) %collective-permute-start.2) | collective-permute-done | bytes 266272 | tf_op jit(solution)/shard_map/spread_01/ppermute | solution.py:404
  23.2 4.3 %collective-permute-start.4 = (f32[2080,128]{1,0:T(8,128)}, f32[2080,128]{1,0:T(8,128)}, u32[]{:S(2)}, u32[]{:S(2)}) collective-permute-start(f32[2080,128]{1,0:T(8,128)} %joined.1.a_refs_0__0_), channel_id=1, source_target_pairs={{0,2},{2,0},{4,6},{6,4},{1,3},{3,1},{5,7},{7,5},{8,10},{10,8},{12,... | collective-permute-start | bytes 3194888 | tf_op jit(solution)/shard_map/near/ppermute | solution.py:350
  28.9 10.0 %placed_00.1 = (f32[8,64,384]{2,1,0:T(8,128)}, f32[8,64,384]{2,1,0:T(8,128)S(1)}) custom-call(s32[2440]{0:T(1024)S(1)} %concatenate.16.table, f32[2080,128]{1,0:T(8,128)} %joined.1.a_refs_0__0_, f32[16384,256]{1,0:T(8,128)} %bitcast.36, f32[16384,256]{1,0:T(8,128)} %collective-permute-done.5.b_mate), custom_call_target="tpu_custom_call" | custom-call | flops 16000000000 | bytes 2621440 | tf_op jit(solution)/shard_map/placed_00/pallas_call | solution.py:192
  41.3 10.7 %collective-permute-done.4.value = f32[2080,128]{1,0:T(8,128)} collective-permute-done((f32[2080,128]{1,0:T(8,128)}, f32[2080,128]{1,0:T(8,128)}, u32[]{:S(2)}, u32[]{:S(2)}) %collective-permute-start.4) | collective-permute-done | bytes 1064992 | tf_op jit(solution)/shard_map/near/ppermute | solution.py:350
  52.7 9.2 %placed_10.1 = (f32[8,64,384]{2,1,0:T(8,128)S(1)}, f32[8,64,384]{2,1,0:T(8,128)S(1)}) custom-call(s32[2440]{0:T(1024)S(1)} %concatenate.16.table, f32[2080,128]{1,0:T(8,128)} %shard_map.55.a_refs_0__0_, f32[16384,256]{1,0:T(8,128)} %bitcast.37, f32[16384,256]{1,0:T(8,128)} %collective-permute-done.5.b_mate, f32[8,64,384]{2,1,0:T(8,128)S(1)} %copy-done.1), custom_call_target="tpu_custom_call" | custom-call | flops 16000000000 | bytes 2621440 | tf_op jit(solution)/shard_map/placed_10/pallas_call | solution.py:192
  62.0 1.6 collective-permute-start.19
  63.5 11.6 %collective-permute-done.8.after_1_.a_refs_0__0_ = f32[2080,128]{1,0:T(8,128)S(1)} collective-permute-done((f32[2080,128]{1,0:T(8,128)S(1)}, f32[2080,128]{1,0:T(8,128)S(1)}, u32[]{:S(2)}, u32[]{:S(2)}) %collective-permute-start.8) | collective-permute-done | bytes 1064992 | tf_op jit(solution)/shard_map/outer/ppermute | solution.py:350
  75.2 4.7 %placed_20.1 = (f32[4,64,384]{2,1,0:T(8,128)S(1)}, f32[4,64,384]{2,1,0:T(8,128)S(1)}) custom-call(s32[2440]{0:T(1024)S(1)} %concatenate.16.table, f32[2080,128]{1,0:T(8,128)S(1)} %collective-permute-done.8.after_1_.a_refs_0__0_, f32[2080,128]{1,0:T(8,128)S(1)} %collective-permute-done.7.a_refs_1__0_, f32[16384,256]{1,0:T(8,128)} %bitcast.38, ...), custom_call_target="tpu_custom_call" | custom-call | flops 8000000000 | bytes 1835008 | tf_op jit(solution)/shard_map/placed_20/pallas_call | solution.py:192
  81.9 4.7 %placed_21.1 = (f32[4,64,384]{2,1,0:T(8,128)S(1)}, f32[4,64,384]{2,1,0:T(8,128)S(1)}) custom-call(s32[2440]{0:T(1024)S(1)} %concatenate.16.table, f32[2080,128]{1,0:T(8,128)S(1)} %collective-permute-done.8.after_1_.a_refs_0__0_, f32[2080,128]{1,0:T(8,128)S(1)} %collective-permute-done.7.a_refs_1__0_, f32[16384,256]{1,0:T(8,128)} %bitcast.39, ...), custom_call_target="tpu_custom_call" | custom-call | flops 8000000000 | bytes 1835008 | tf_op jit(solution)/shard_map/placed_21/pallas_call | solution.py:192
  86.7 1.6 collective-permute-start.15
  92.7 10.7 %collective-permute-done.10.a_refs_0__0_ = f32[1040,128]{1,0:T(8,128)S(1)} collective-permute-done((f32[1040,128]{1,0:T(8,128)S(1)}, f32[1040,128]{1,0:T(8,128)S(1)}, u32[]{:S(2)}, u32[]{:S(2)}) %collective-permute-start.10) | collective-permute-done | bytes 532512 | tf_op jit(solution)/shard_map/last/ppermute | solution.py:350
  104.7 4.7 %placed_30.1 = (f32[4,64,384]{2,1,0:T(8,128)S(1)}, f32[4,64,384]{2,1,0:T(8,128)S(1)}) custom-call(s32[2440]{0:T(1024)S(1)} %concatenate.16.table, f32[1040,128]{1,0:T(8,128)S(1)} %collective-permute-done.10.a_refs_0__0_, f32[1040,128]{1,0:T(8,128)S(1)} %get-tuple-element.22.a_refs_1__0_, f32[16384,256]{1,0:T(8,128)} %bitcast.40, ...), custom_call_target="tpu_custom_call" | custom-call | flops 8000000000 | bytes 1310720 | tf_op jit(solution)/shard_map/placed_30/pallas_call | solution.py:192
  109.3 7.3 %collective-permute-done.9.a_refs_0__0_ = f32[1040,128]{1,0:T(8,128)S(1)} collective-permute-done((f32[1040,128]{1,0:T(8,128)S(1)}, f32[1040,128]{1,0:T(8,128)S(1)}, u32[]{:S(2)}, u32[]{:S(2)}) %collective-permute-start.9) | collective-permute-done | bytes 532512 | tf_op jit(solution)/shard_map/last/ppermute | solution.py:350
  117.2 4.7 %placed_31.1 = (f32[4,64,384]{2,1,0:T(8,128)S(1)}, f32[4,64,384]{2,1,0:T(8,128)S(1)}) custom-call(s32[2440]{0:T(1024)S(1)} %concatenate.16.table, f32[1040,128]{1,0:T(8,128)S(1)} %collective-permute-done.9.a_refs_0__0_, f32[1040,128]{1,0:T(8,128)S(1)} %get-tuple-element.21.a_refs_1__0_, f32[16384,256]{1,0:T(8,128)} %bitcast.41, ...), custom_call_target="tpu_custom_call" | custom-call | flops 8000000000 | bytes 1310720 | tf_op jit(solution)/shard_map/placed_31/pallas_call | solution.py:192
  123.4 3.1 %collective-permute-start.18 = (f32[4,64,384]{2,1,0:T(8,128)S(1)}, f32[4,64,384]{2,1,0:T(8,128)S(1)}, u32[]{:S(2)}, u32[]{:S(2)}) collective-permute-start(f32[4,64,384]{2,1,0:T(8,128)S(1)} %sum_20.1.total), channel_id=1, source_target_pairs={{0,1},{2,3},{5,4},{7,6},{8,9},{10,11},{13,12},{15,14},{16,17},{18,... | collective-permute-start | bytes 1179656 | tf_op jit(solution)/shard_map/y_20/ppermute | solution.py:467
  126.6 1.6 %collective-permute-done.13.two = f32[4,64,384]{2,1,0:T(8,128)S(1)} collective-permute-done((f32[4,64,384]{2,1,0:T(8,128)S(1)}, f32[4,64,384]{2,1,0:T(8,128)S(1)}, u32[]{:S(2)}, u32[]{:S(2)}) %collective-permute-start.13) | collective-permute-done | bytes 393248 | tf_op jit(solution)/shard_map/x_30/ppermute | solution.py:452
  128.2 2.3 %collective-permute-start.16 = (f32[4,64,384]{2,1,0:T(8,128)S(1)}, f32[4,64,384]{2,1,0:T(8,128)S(1)}, u32[]{:S(2)}, u32[]{:S(2)}) collective-permute-start(f32[4,64,384]{2,1,0:T(8,128)S(1)} %sum_21.1.total), channel_id=1, source_target_pairs={{0,1},{2,3},{5,4},{7,6},{8,9},{10,11},{13,12},{15,14},{16,17},{18,... | collective-permute-start | bytes 1179656 | tf_op jit(solution)/shard_map/y_21/ppermute | solution.py:467
  130.5 2.3 %collective-permute-done.11.two = f32[4,64,384]{2,1,0:T(8,128)S(1)} collective-permute-done((f32[4,64,384]{2,1,0:T(8,128)S(1)}, f32[4,64,384]{2,1,0:T(8,128)S(1)}, u32[]{:S(2)}, u32[]{:S(2)}) %collective-permute-start.11) | collective-permute-done | bytes 393248 | tf_op jit(solution)/shard_map/x_31/ppermute | solution.py:452
  132.8 3.1 %collective-permute-start.14 = (f32[4,64,384]{2,1,0:T(8,128)S(1)}, f32[4,64,384]{2,1,0:T(8,128)S(1)}, u32[]{:S(2)}, u32[]{:S(2)}) collective-permute-start(f32[4,64,384]{2,1,0:T(8,128)S(1)} %sum_30.1.total), channel_id=1, source_target_pairs={{0,1},{2,3},{5,4},{7,6},{8,9},{10,11},{13,12},{15,14},{16,17},{18,... | collective-permute-start | bytes 1179656 | tf_op jit(solution)/shard_map/y_30/ppermute | solution.py:467
  140.9 3.6 %collective-permute-done.16.other = f32[4,64,384]{2,1,0:T(8,128)S(1)} collective-permute-done((f32[4,64,384]{2,1,0:T(8,128)S(1)}, f32[4,64,384]{2,1,0:T(8,128)S(1)}, u32[]{:S(2)}, u32[]{:S(2)}) %collective-permute-start.16) | collective-permute-done | bytes 393248 | tf_op jit(solution)/shard_map/y_21/ppermute | solution.py:467
  145.1 7.2 %collective-permute-done.14.other = f32[4,64,384]{2,1,0:T(8,128)S(1)} collective-permute-done((f32[4,64,384]{2,1,0:T(8,128)S(1)}, f32[4,64,384]{2,1,0:T(8,128)S(1)}, u32[]{:S(2)}, u32[]{:S(2)}) %collective-permute-start.14) | collective-permute-done | bytes 393248 | tf_op jit(solution)/shard_map/y_30/ppermute | solution.py:467
  152.8 3.6 %collective-permute-done.12.other = f32[4,64,384]{2,1,0:T(8,128)S(1)} collective-permute-done((f32[4,64,384]{2,1,0:T(8,128)S(1)}, f32[4,64,384]{2,1,0:T(8,128)S(1)}, u32[]{:S(2)}, u32[]{:S(2)}) %collective-permute-start.12) | collective-permute-done | bytes 393248 | tf_op jit(solution)/shard_map/y_31/ppermute | solution.py:467
  (73 shorter events, 28.5 us)
Async XLA Ops:
  0.0 28.9 %collective-permute-start.5 = (f32[16384,256]{1,0:T(8,128)}, f32[16384,256]{1,0:T(8,128)}, u32[]{:S(2)}, u32[]{:S(2)}) collective-permute-start(f32[16384,256]{1,0:T(8,128)} %bitcast.35), channel_id=1, source_target_pairs={{0,8},{8,0},{16,24},{24,16},{1,9},{9,1},{17,25},{25,17},{2,10},{10... | collective-permute-start | bytes 50331656 | tf_op jit(solution)/shard_map/mate/ppermute | solution.py:375
  4.3 18.4 %copy-start.2 = (s32[256,1,4]{0,2,1:T(4,128)S(1)}, s32[256,1,4]{0,2,1:T(4,128)}, u32[]{:S(2)}) copy-start(s32[256,1,4]{0,2,1:T(4,128)} %param.8) | copy-start | bytes 12292
  4.3 10.8 %collective-permute-start.3 = (f32[520,128]{1,0:T(8,128)S(1)}, f32[520,128]{1,0:T(8,128)S(1)}, u32[]{:S(2)}, u32[]{:S(2)}) collective-permute-start(f32[520,128]{1,0:T(8,128)S(1)} %get-tuple-element.41), channel_id=1, source_target_pairs={{0,17},{1,16},{8,25},{9,24},{16,1},{17,0},{24,9},{25,8},{2,19},{3,... | collective-permute-start | bytes 798728 | tf_op jit(solution)/shard_map/spread_11/ppermute | solution.py:404
  7.8 12.8 %collective-permute-start.2 = (f32[520,128]{1,0:T(8,128)S(1)}, f32[520,128]{1,0:T(8,128)S(1)}, u32[]{:S(2)}, u32[]{:S(2)}) collective-permute-start(f32[520,128]{1,0:T(8,128)S(1)} %get-tuple-element.43), channel_id=1, source_target_pairs={{0,1},{1,0},{8,9},{9,8},{16,17},{17,16},{24,25},{25,24},{2,3},{3,2... | collective-permute-start | bytes 798728 | tf_op jit(solution)/shard_map/spread_01/ppermute | solution.py:404
  8.3 12.6 %collective-permute-start.1 = (f32[520,128]{1,0:T(8,128)S(1)}, f32[520,128]{1,0:T(8,128)S(1)}, u32[]{:S(2)}, u32[]{:S(2)}) collective-permute-start(f32[520,128]{1,0:T(8,128)S(1)} %get-tuple-element.44), channel_id=1, source_target_pairs={{0,16},{1,17},{8,24},{9,25},{16,0},{17,1},{24,8},{25,9},{2,18},{3,... | collective-permute-start | bytes 798728 | tf_op jit(solution)/shard_map/spread_10/ppermute | solution.py:404
  22.0 5.6 %collective-permute-start.7 = (f32[2080,128]{1,0:T(8,128)}, f32[2080,128]{1,0:T(8,128)S(1)}, u32[]{:S(2)}, u32[]{:S(2)}) collective-permute-start(f32[2080,128]{1,0:T(8,128)} %joined.1.a_refs_0__0_), channel_id=1, source_target_pairs={{2,4},{4,2},{3,5},{5,3},{10,12},{12,10},{11,13},{13,11},{18,20},{2... | collective-permute-start | bytes 3194888 | tf_op jit(solution)/shard_map/inner/ppermute | solution.py:350
  23.0 4.5 %collective-permute-start = (s32[1024]{0:T(1024)S(1)}, s32[1024]{0:T(1024)S(1)}, u32[]{:S(2)}, u32[]{:S(2)}) collective-permute-start(s32[1024]{0:T(1024)S(1)} %reshape.69), channel_id=1, source_target_pairs={{0,8},{8,0},{16,24},{24,16},{1,9},{9,1},{17,25},{25,17},{2,10},{10... | collective-permute-start | bytes 12296 | tf_op jit(solution)/shard_map/mate_index/ppermute | solution.py:377
  23.2 28.8 %collective-permute-start.4 = (f32[2080,128]{1,0:T(8,128)}, f32[2080,128]{1,0:T(8,128)}, u32[]{:S(2)}, u32[]{:S(2)}) collective-permute-start(f32[2080,128]{1,0:T(8,128)} %joined.1.a_refs_0__0_), channel_id=1, source_target_pairs={{0,2},{2,0},{4,6},{6,4},{1,3},{3,1},{5,7},{7,5},{8,10},{10,8},{12,... | collective-permute-start | bytes 3194888 | tf_op jit(solution)/shard_map/near/ppermute | solution.py:350
  27.6 47.5 %collective-permute-start.8 = (f32[2080,128]{1,0:T(8,128)S(1)}, f32[2080,128]{1,0:T(8,128)S(1)}, u32[]{:S(2)}, u32[]{:S(2)}) collective-permute-start(f32[2080,128]{1,0:T(8,128)S(1)} %collective-permute-done.7.a_refs_1__0_), channel_id=1, source_target_pairs={{2,0},{4,6},{3,1},{5,7},{10,8},{12,14},{11,9},{13,15},{18,16},{20,... | collective-permute-start | bytes 3194888 | tf_op jit(solution)/shard_map/outer/ppermute | solution.py:350
  39.8 50.4 %collective-permute-start.21 = (f32[8,64,384]{2,1,0:T(8,128)}, f32[8,64,384]{2,1,0:T(8,128)}, u32[]{:S(2)}, u32[]{:S(2)}) collective-permute-start(f32[8,64,384]{2,1,0:T(8,128)} %get-tuple-element.32), channel_id=1, source_target_pairs={{0,16},{8,24},{16,0},{24,8},{1,17},{9,25},{17,1},{25,9},{2,18},{10... | collective-permute-start | bytes 2359304 | tf_op jit(solution)/shard_map/x_00/ppermute | solution.py:452
  52.0 27.9 %collective-permute-start.6 = (f32[2080,128]{1,0:T(8,128)}, f32[2080,128]{1,0:T(8,128)S(1)}, u32[]{:S(2)}, u32[]{:S(2)}) collective-permute-start(f32[2080,128]{1,0:T(8,128)} %shard_map.55.a_refs_0__0_), channel_id=1, source_target_pairs={{4,2},{2,4},{5,3},{3,5},{12,10},{10,12},{13,11},{11,13},{20,18},{1... | collective-permute-start | bytes 3194888 | tf_op jit(solution)/shard_map/through/ppermute | solution.py:350
  62.0 26.8 %collective-permute-start.19 = (f32[8,64,384]{2,1,0:T(8,128)S(1)}, f32[8,64,384]{2,1,0:T(8,128)S(1)}, u32[]{:S(2)}, u32[]{:S(2)}) collective-permute-start(f32[8,64,384]{2,1,0:T(8,128)S(1)} %get-tuple-element.31), channel_id=1, source_target_pairs={{0,16},{8,24},{16,0},{24,8},{1,17},{9,25},{17,1},{25,9},{2,18},{10... | collective-permute-start | bytes 2359304 | tf_op jit(solution)/shard_map/x_10/ppermute | solution.py:452
  80.6 22.8 %collective-permute-start.10 = (f32[1040,128]{1,0:T(8,128)S(1)}, f32[1040,128]{1,0:T(8,128)S(1)}, u32[]{:S(2)}, u32[]{:S(2)}) collective-permute-start(f32[1040,128]{1,0:T(8,128)S(1)} %get-tuple-element.22.a_refs_1__0_), channel_id=1, source_target_pairs={{2,0},{4,6},{3,1},{5,7},{10,8},{12,14},{11,9},{13,15},{18,16},{20,... | collective-permute-start | bytes 1597448 | tf_op jit(solution)/shard_map/last/ppermute | solution.py:350
  86.7 36.8 %collective-permute-start.15 = (f32[4,64,384]{2,1,0:T(8,128)S(1)}, f32[4,64,384]{2,1,0:T(8,128)S(1)}, u32[]{:S(2)}, u32[]{:S(2)}) collective-permute-start(f32[4,64,384]{2,1,0:T(8,128)S(1)} %get-tuple-element.29), channel_id=1, source_target_pairs={{0,16},{8,24},{16,0},{24,8},{1,17},{9,25},{17,1},{25,9},{2,18},{10... | collective-permute-start | bytes 1179656 | tf_op jit(solution)/shard_map/x_21/ppermute | solution.py:452
  88.2 33.6 %collective-permute-start.17 = (f32[4,64,384]{2,1,0:T(8,128)S(1)}, f32[4,64,384]{2,1,0:T(8,128)S(1)}, u32[]{:S(2)}, u32[]{:S(2)}) collective-permute-start(f32[4,64,384]{2,1,0:T(8,128)S(1)} %get-tuple-element.30), channel_id=1, source_target_pairs={{0,16},{8,24},{16,0},{24,8},{1,17},{9,25},{17,1},{25,9},{2,18},{10... | collective-permute-start | bytes 1179656 | tf_op jit(solution)/shard_map/x_20/ppermute | solution.py:452
  88.9 50.0 %collective-permute-start.20 = (f32[8,64,384]{2,1,0:T(8,128)S(1)}, f32[8,64,384]{2,1,0:T(8,128)S(1)}, u32[]{:S(2)}, u32[]{:S(2)}) collective-permute-start(f32[8,64,384]{2,1,0:T(8,128)S(1)} %sum_10.1.total), channel_id=1, source_target_pairs={{1,0},{3,2},{4,5},{6,7},{9,8},{11,10},{12,13},{14,15},{17,16},{19,... | collective-permute-start | bytes 2359304 | tf_op jit(solution)/shard_map/y_10/ppermute | solution.py:467
  91.4 44.6 %collective-permute-start.22 = (f32[8,64,384]{2,1,0:T(8,128)S(1)}, f32[8,64,384]{2,1,0:T(8,128)S(1)}, u32[]{:S(2)}, u32[]{:S(2)}) collective-permute-start(f32[8,64,384]{2,1,0:T(8,128)S(1)} %sum_00.1.total), channel_id=1, source_target_pairs={{1,0},{3,2},{4,5},{6,7},{9,8},{11,10},{12,13},{14,15},{17,16},{19,... | collective-permute-start | bytes 2359304 | tf_op jit(solution)/shard_map/y_00/ppermute | solution.py:467
  103.4 13.2 %collective-permute-start.9 = (f32[1040,128]{1,0:T(8,128)S(1)}, f32[1040,128]{1,0:T(8,128)S(1)}, u32[]{:S(2)}, u32[]{:S(2)}) collective-permute-start(f32[1040,128]{1,0:T(8,128)S(1)} %get-tuple-element.21.a_refs_1__0_), channel_id=1, source_target_pairs={{2,0},{4,6},{3,1},{5,7},{10,8},{12,14},{11,9},{13,15},{18,16},{20,... | collective-permute-start | bytes 1597448 | tf_op jit(solution)/shard_map/last/ppermute | solution.py:350
  116.6 11.6 %collective-permute-start.13 = (f32[4,64,384]{2,1,0:T(8,128)S(1)}, f32[4,64,384]{2,1,0:T(8,128)S(1)}, u32[]{:S(2)}, u32[]{:S(2)}) collective-permute-start(f32[4,64,384]{2,1,0:T(8,128)S(1)} %get-tuple-element.28), channel_id=1, source_target_pairs={{0,16},{8,24},{16,0},{24,8},{1,17},{9,25},{17,1},{25,9},{2,18},{10... | collective-permute-start | bytes 1179656 | tf_op jit(solution)/shard_map/x_30/ppermute | solution.py:452
  121.9 11.0 %collective-permute-start.11 = (f32[4,64,384]{2,1,0:T(8,128)S(1)}, f32[4,64,384]{2,1,0:T(8,128)S(1)}, u32[]{:S(2)}, u32[]{:S(2)}) collective-permute-start(f32[4,64,384]{2,1,0:T(8,128)S(1)} %get-tuple-element.27), channel_id=1, source_target_pairs={{0,16},{8,24},{16,0},{24,8},{1,17},{9,25},{17,1},{25,9},{2,18},{10... | collective-permute-start | bytes 1179656 | tf_op jit(solution)/shard_map/x_31/ppermute | solution.py:452
  123.4 16.9 %collective-permute-start.18 = (f32[4,64,384]{2,1,0:T(8,128)S(1)}, f32[4,64,384]{2,1,0:T(8,128)S(1)}, u32[]{:S(2)}, u32[]{:S(2)}) collective-permute-start(f32[4,64,384]{2,1,0:T(8,128)S(1)} %sum_20.1.total), channel_id=1, source_target_pairs={{0,1},{2,3},{5,4},{7,6},{8,9},{10,11},{13,12},{15,14},{16,17},{18,... | collective-permute-start | bytes 1179656 | tf_op jit(solution)/shard_map/y_20/ppermute | solution.py:467
  128.2 16.3 %collective-permute-start.16 = (f32[4,64,384]{2,1,0:T(8,128)S(1)}, f32[4,64,384]{2,1,0:T(8,128)S(1)}, u32[]{:S(2)}, u32[]{:S(2)}) collective-permute-start(f32[4,64,384]{2,1,0:T(8,128)S(1)} %sum_21.1.total), channel_id=1, source_target_pairs={{0,1},{2,3},{5,4},{7,6},{8,9},{10,11},{13,12},{15,14},{16,17},{18,... | collective-permute-start | bytes 1179656 | tf_op jit(solution)/shard_map/y_21/ppermute | solution.py:467
  132.8 19.5 %collective-permute-start.14 = (f32[4,64,384]{2,1,0:T(8,128)S(1)}, f32[4,64,384]{2,1,0:T(8,128)S(1)}, u32[]{:S(2)}, u32[]{:S(2)}) collective-permute-start(f32[4,64,384]{2,1,0:T(8,128)S(1)} %sum_30.1.total), channel_id=1, source_target_pairs={{0,1},{2,3},{5,4},{7,6},{8,9},{10,11},{13,12},{15,14},{16,17},{18,... | collective-permute-start | bytes 1179656 | tf_op jit(solution)/shard_map/y_30/ppermute | solution.py:467
  136.0 20.5 %collective-permute-start.12 = (f32[4,64,384]{2,1,0:T(8,128)S(1)}, f32[4,64,384]{2,1,0:T(8,128)S(1)}, u32[]{:S(2)}, u32[]{:S(2)}) collective-permute-start(f32[4,64,384]{2,1,0:T(8,128)S(1)} %sum_31.1.total), channel_id=1, source_target_pairs={{0,1},{2,3},{5,4},{7,6},{8,9},{10,11},{13,12},{15,14},{16,17},{18,... | collective-permute-start | bytes 1179656 | tf_op jit(solution)/shard_map/y_31/ppermute | solution.py:467
  (2 other events, 13.8 us)

commit v3 on v2

--- a/solution.py
+++ b/solution.py
@@ -12,8 +12,10 @@
 COST = 1000000000
 VMEM_BYTES = 48 * 1024 * 1024
 CUTS = (1, 1, 2, 2)
-Y_WITH = {0: 1, 1: 3, 2: 4, 3: 5, 4: 5, 5: 5}
-SETTLE = {6: [0, 1, 2, 3, 4, 5]}
+Y_WITH = {0: 1, 1: 2, 2: 3, 3: 4, 4: 5, 5: 5}
+BEFORE_SUM = {5: [2]}
+BEFORE_OTHER = {4: [0]}
+SUM_AFTER = {4: [1, 2], 5: [3]}
 
 
 def slot_piece(slot, z, tiles):
@@ -304,37 +306,29 @@
     )(one, two, after)
 
 
-def split_kernel(halves, depths, cuts, meta, value, after, *refs):
-    outs, sem = refs[:cuts], refs[cuts]
+def taken_kernel(halves, depths, cuts, cut, meta, value, after, out, sem):
     y = meta[2]
-    across = depths // cuts
     length = value.shape[0] // (halves * cuts)
     copies = []
     for ex in range(halves):
-        for cut in range(cuts):
-            at = pl.multiple_of((ex * cuts + jnp.bitwise_xor(y // across, cut)) * length, 8)
-            copies.append(
-                pltpu.make_async_copy(
-                    value.at[pl.ds(at, length)], outs[cut].at[pl.ds(ex * length, length)], sem.at[ex, cut]
-                )
-            )
+        at = pl.multiple_of((ex * cuts + jnp.bitwise_xor(y // (depths // cuts), cut)) * length, 8)
+        copies.append(pltpu.make_async_copy(value.at[pl.ds(at, length)], out.at[pl.ds(ex * length, length)], sem.at[ex]))
     for copy in copies:
         copy.start()
     for copy in copies:
         copy.wait()
 
 
-def split(halves, depths, cuts, meta, value, after):
+def taken(halves, depths, cuts, cut, meta, value, after):
     anywhere = pl.BlockSpec(memory_space=pl.ANY)
-    shape = jax.ShapeDtypeStruct((value.shape[0] // cuts, value.shape[1]), value.dtype)
-    return pl.pallas_call(
-        functools.partial(split_kernel, halves, depths, cuts),
-        out_shape=(shape,) * cuts,
+    return pl.pallas_call(
+        functools.partial(taken_kernel, halves, depths, cuts, cut),
+        out_shape=jax.ShapeDtypeStruct((value.shape[0] // cuts, value.shape[1]), value.dtype),
         in_specs=[pl.BlockSpec(memory_space=pltpu.SMEM), anywhere, [anywhere] * len(after)],
-        out_specs=(pl.BlockSpec(memory_space=pltpu.VMEM),) * cuts,
-        scratch_shapes=[pltpu.SemaphoreType.DMA((halves, cuts))],
+        out_specs=pl.BlockSpec(memory_space=pltpu.VMEM),
+        scratch_shapes=[pltpu.SemaphoreType.DMA((halves,))],
         compiler_params=pltpu.CompilerParams(vmem_limit_bytes=VMEM_BYTES),
-        cost_estimate=pl.CostEstimate(flops=0, bytes_accessed=8 * value.size, transcendentals=0),
+        cost_estimate=pl.CostEstimate(flops=0, bytes_accessed=8 * value.size // cuts, transcendentals=0),
     )(meta, value, after)
 
 
@@ -423,14 +417,16 @@
         if slot == 0:
             a_sources = [[[here]]]
         elif slot == 1:
-            near = gated(near, order)
+            inner = gated(inner, order)
+            near = gated(near, order + [inner])
             outer, through = along(inner, "outer"), along(near, "through")
             a_sources = [[[near]]]
         elif slot == 2:
             a_sources = [[[outer], [inner]]]
-            throughs = split(halves, depths, CUTS[3], meta, through, order + [outer])
+            throughs = [taken(halves, depths, CUTS[3], 0, meta, through, order + [outer])]
+            order = order + throughs
+        else:
             lasts = [along(value, "last") for value in throughs]
-        else:
             a_sources = [[[there], [here]] for there, here in zip(lasts, throughs)]
         cuts = CUTS[slot]
         count = per_piece // cuts
@@ -439,15 +435,17 @@
         for cut in range(cuts):
             after = list(order)
             if depths == 2:
-                for n in SETTLE.get(number, []):
-                    out = settled(*settle[n], out)
-                    after.append(out)
+                after += [settle[n][6] for n in BEFORE_SUM.get(number, [])]
+                after += [settle[n][7] for n in BEFORE_OTHER.get(number, [])]
             across_here = depths if len(a_sources) == 1 else depths // cuts
             with jax.named_scope(f"placed_{slot}{cut}"):
                 send, keep = placed_products(
                     dims, slot, cut * count, count, across_here, whole_table, a_sources[cut % len(a_sources)], b_own, b_mate, after
                 )
             order = [keep]
+            if slot == 2 and cut == 0:
+                throughs += [taken(halves, depths, CUTS[3], n, meta, through, order) for n in range(1, CUTS[3])]
+                order = order + throughs[1:]
             with jax.named_scope(f"x_{slot}{cut}"):
                 other = lax.ppermute(send, "row", across)
             x_sums.append((keep, other))
@@ -462,15 +460,15 @@
                     pending.remove(item)
                     n, its_slot, its_cut, its_count, its_perm = item
                     with jax.named_scope(f"sum_{its_slot}{its_cut}"):
-                        total = summed(*x_sums[n], order)
+                        total = summed(*x_sums[n], order + [settle[m][7] for m in SUM_AFTER.get(n, [])])
                     with jax.named_scope(f"y_{its_slot}{its_cut}"):
                         other = lax.ppermute(total, ("col", "depth"), its_perm)
                     settle[n] = (its_slot, its_cut * its_count, depths, steps, tiles, meta, total, other)
             number += 1
 
     if depths == 2:
-        for n in SETTLE[number]:
-            out = settled(*settle[n], out)
+        for one in settle:
+            out = settled(*one, out)
     if depths != 2:
         full = jnp.zeros((tiles, per_piece) + x_sums[0][0].shape[1:], jnp.float32)
         at = 0

time: 158 us -> 137 us (0.87)
  waiting for transfers between devices: 71 us -> 46.5 us
  starting transfers between devices: 33.9 us -> 37.4 us
  Pallas kernels: 46.6 us -> 44.6 us
    ppermute x6, waiting for transfers between devices: 40.3 us -> 21 us  [along(): return lax.ppermute(value, 'col', pairs[step])]
    ppermute x6, waiting for transfers between devices: 14.4 us -> 5.86 us  [on_device(): other = lax.ppermute(total, ('col', 'depth'), its_perm)]
    ppermute x6, waiting for transfers between devices: 3.9 us -> 7.71 us  [on_device(): other = lax.ppermute(send, 'row', across)]
    ppermute x6, starting transfers between devices: 12.3 us -> 14.7 us  [on_device(): other = lax.ppermute(total, ('col', 'depth'), its_perm)]
    unnamed x9 -> x13, local copies, waits for them, and re-layouts: 2.56 us -> 3.53 us
  transfers between devices with their start and end apart: 23 -> 23, of which waited for: 12 -> 10; matrix products, arithmetic and copies ran while one was open for 3% -> 3% of each run, Pallas kernels for 29% -> 33%
where the time goes in v3:
time: 137 us; the launch traced here: 135 us
  waiting for transfers between devices  46.5 us (34%)
  Pallas kernels  44.6 us (33%)
  starting transfers between devices  37.4 us (27%)
  local copies, waits for them, and re-layouts  5.91 us (4%)
    pallas_call x6, Pallas kernels, placed_products(): pl.pallas_call(functools.partial(placed_kernel, dims, slot, first, count,...  36.5 us
    ppermute x6, waiting for transfers between devices, along(): return lax.ppermute(value, 'col', pairs[step])  21 us
    ppermute x6, starting transfers between devices, on_device(): other = lax.ppermute(total, ('col', 'depth'), its_perm)  14.7 us
    ppermute x3, waiting for transfers between devices, on_device(): others.append(lax.ppermute(a_for(ex, e), ('row', 'depth'), perm))  12 us
    ppermute x6, starting transfers between devices, along(): return lax.ppermute(value, 'col', pairs[step])  9.84 us
    ppermute x6, starting transfers between devices, on_device(): other = lax.ppermute(send, 'row', across)  8.19 us
    ppermute x6, waiting for transfers between devices, on_device(): other = lax.ppermute(send, 'row', across)  7.71 us
    ppermute x6, waiting for transfers between devices, on_device(): other = lax.ppermute(total, ('col', 'depth'), its_perm)  5.86 us
  transfers between devices with their start and end apart: 23, of which 10 were waited for; matrix products, arithmetic and copies ran while one was open for 3% of the time, Pallas kernels for 33%

profile of v3, /device:TPU:0, one launch (start us, length us, event | category | flops | bytes accessed | tf_op | source)
XLA Modules:
  0.0 135.1 jit_solution(16940782613778177941)
XLA Ops:
  4.3 3.5 %collective-permute-start.3 = (f32[520,128]{1,0:T(8,128)S(1)}, f32[520,128]{1,0:T(8,128)S(1)}, u32[]{:S(2)}, u32[]{:S(2)}) collective-permute-start(f32[520,128]{1,0:T(8,128)S(1)} %get-tuple-element.37), channel_id=1, source_target_pairs={{0,17},{1,16},{8,25},{9,24},{16,1},{17,0},{24,9},{25,8},{2,19},{3,... | collective-permute-start | bytes 798728 | tf_op jit(solution)/shard_map/spread_11/ppermute | solution.py:398
  8.9 6.2 %collective-permute-done.3.parts_3_ = f32[520,128]{1,0:T(8,128)S(1)} collective-permute-done((f32[520,128]{1,0:T(8,128)S(1)}, f32[520,128]{1,0:T(8,128)S(1)}, u32[]{:S(2)}, u32[]{:S(2)}) %collective-permute-start.3) | collective-permute-done | bytes 266272 | tf_op jit(solution)/shard_map/spread_11/ppermute | solution.py:398
  15.1 5.5 %collective-permute-done.2.parts_1_ = f32[520,128]{1,0:T(8,128)S(1)} collective-permute-done((f32[520,128]{1,0:T(8,128)S(1)}, f32[520,128]{1,0:T(8,128)S(1)}, u32[]{:S(2)}, u32[]{:S(2)}) %collective-permute-start.2) | collective-permute-done | bytes 266272 | tf_op jit(solution)/shard_map/spread_01/ppermute | solution.py:398
  21.8 4.4 %collective-permute-start.4 = (f32[2080,128]{1,0:T(8,128)S(1)}, f32[2080,128]{1,0:T(8,128)}, u32[]{:S(2)}, u32[]{:S(2)}) collective-permute-start(f32[2080,128]{1,0:T(8,128)S(1)} %joined.1.a_refs_0__0_), channel_id=1, source_target_pairs={{0,2},{2,0},{4,6},{6,4},{1,3},{3,1},{5,7},{7,5},{8,10},{10,8},{12,... | collective-permute-start | bytes 3194888 | tf_op jit(solution)/shard_map/near/ppermute | solution.py:344
  26.3 8.4 %placed_00.1 = (f32[8,64,384]{2,1,0:T(8,128)}, f32[8,64,384]{2,1,0:T(8,128)S(1)}) custom-call(s32[2440]{0:T(1024)S(1)} %concatenate.16.table, f32[2080,128]{1,0:T(8,128)S(1)} %joined.1.a_refs_0__0_, f32[16384,256]{1,0:T(8,128)} %bitcast.36, f32[16384,256]{1,0:T(8,128)} %collective-permute-done.5.b_mate), custom_call_target="tpu_custom_call" | custom-call | flops 16000000000 | bytes 2621440 | tf_op jit(solution)/shard_map/placed_00/pallas_call | solution.py:194
  35.5 2.2 %collective-permute-start.11 = (f32[8,64,384]{2,1,0:T(8,128)}, f32[8,64,384]{2,1,0:T(8,128)}, u32[]{:S(2)}, u32[]{:S(2)}) collective-permute-start(f32[8,64,384]{2,1,0:T(8,128)} %get-tuple-element.21), channel_id=1, source_target_pairs={{0,16},{8,24},{16,0},{24,8},{1,17},{9,25},{17,1},{25,9},{2,18},{10... | collective-permute-start | bytes 2359304 | tf_op jit(solution)/shard_map/x_00/ppermute | solution.py:450
  40.1 9.5 %collective-permute-done.4.value = f32[2080,128]{1,0:T(8,128)} collective-permute-done((f32[2080,128]{1,0:T(8,128)S(1)}, f32[2080,128]{1,0:T(8,128)}, u32[]{:S(2)}, u32[]{:S(2)}) %collective-permute-start.4) | collective-permute-done | bytes 1064992 | tf_op jit(solution)/shard_map/near/ppermute | solution.py:344
  50.3 9.2 %placed_10.1 = (f32[8,64,384]{2,1,0:T(8,128)S(1)}, f32[8,64,384]{2,1,0:T(8,128)S(1)}) custom-call(s32[2440]{0:T(1024)S(1)} %concatenate.16.table, f32[2080,128]{1,0:T(8,128)} %shard_map.56.a_refs_0__0_, f32[16384,256]{1,0:T(8,128)} %bitcast.37, f32[16384,256]{1,0:T(8,128)} %collective-permute-done.5.b_mate, f32[8,64,384]{2,1,0:T(8,128)S(1)} %copy-done.3), custom_call_target="tpu_custom_call" | custom-call | flops 16000000000 | bytes 2621440 | tf_op jit(solution)/shard_map/placed_10/pallas_call | solution.py:194
  59.6 1.6 %collective-permute-start.19 = (f32[8,64,384]{2,1,0:T(8,128)S(1)}, f32[8,64,384]{2,1,0:T(8,128)S(1)}, u32[]{:S(2)}, u32[]{:S(2)}) collective-permute-start(f32[8,64,384]{2,1,0:T(8,128)S(1)} %get-tuple-element.28), channel_id=1, source_target_pairs={{0,16},{8,24},{16,0},{24,8},{1,17},{9,25},{17,1},{25,9},{2,18},{10... | collective-permute-start | bytes 2359304 | tf_op jit(solution)/shard_map/x_10/ppermute | solution.py:450
  63.8 11.5 %collective-permute-done.8.after_1_.a_refs_0__0_ = f32[2080,128]{1,0:T(8,128)S(1)} collective-permute-done((f32[2080,128]{1,0:T(8,128)}, f32[2080,128]{1,0:T(8,128)S(1)}, u32[]{:S(2)}, u32[]{:S(2)}) %collective-permute-start.8) | collective-permute-done | bytes 1064992 | tf_op jit(solution)/shard_map/outer/ppermute | solution.py:344
  77.2 4.7 %placed_20.1 = (f32[4,64,384]{2,1,0:T(8,128)S(1)}, f32[4,64,384]{2,1,0:T(8,128)S(1)}) custom-call(s32[2440]{0:T(1024)S(1)} %concatenate.16.table, f32[2080,128]{1,0:T(8,128)S(1)} %collective-permute-done.8.after_1_.a_refs_0__0_, f32[2080,128]{1,0:T(8,128)S(1)} %copy-done.1, f32[16384,256]{1,0:T(8,128)} %bitcast.38, ...), custom_call_target="tpu_custom_call" | custom-call | flops 8000000000 | bytes 1835008 | tf_op jit(solution)/shard_map/placed_20/pallas_call | solution.py:194
  82.0 1.6 %collective-permute-start.13 = (f32[4,64,384]{2,1,0:T(8,128)S(1)}, f32[4,64,384]{2,1,0:T(8,128)S(1)}, u32[]{:S(2)}, u32[]{:S(2)}) collective-permute-start(f32[4,64,384]{2,1,0:T(8,128)S(1)} %get-tuple-element.23), channel_id=1, source_target_pairs={{0,16},{8,24},{16,0},{24,8},{1,17},{9,25},{17,1},{25,9},{2,18},{10... | collective-permute-start | bytes 1179656 | tf_op jit(solution)/shard_map/x_20/ppermute | solution.py:450
  85.5 4.8 %placed_21.1 = (f32[4,64,384]{2,1,0:T(8,128)S(1)}, f32[4,64,384]{2,1,0:T(8,128)S(1)}) custom-call(s32[2440]{0:T(1024)S(1)} %concatenate.16.table, f32[2080,128]{1,0:T(8,128)S(1)} %collective-permute-done.8.after_1_.a_refs_0__0_, f32[2080,128]{1,0:T(8,128)S(1)} %copy-done.1, f32[16384,256]{1,0:T(8,128)} %bitcast.39, ...), custom_call_target="tpu_custom_call" | custom-call | flops 8000000000 | bytes 1835008 | tf_op jit(solution)/shard_map/placed_21/pallas_call | solution.py:194
  93.4 4.9 %collective-permute-start.21 = (f32[4,64,384]{2,1,0:T(8,128)S(1)}, f32[4,64,384]{2,1,0:T(8,128)S(1)}, u32[]{:S(2)}, u32[]{:S(2)}) collective-permute-start(f32[4,64,384]{2,1,0:T(8,128)S(1)} %sum_20.1.after_1_.total), channel_id=1, source_target_pairs={{0,1},{2,3},{5,4},{7,6},{8,9},{10,11},{13,12},{15,14},{16,17},{18,... | collective-permute-start | bytes 1179656 | tf_op jit(solution)/shard_map/y_20/ppermute | solution.py:465
  98.3 4.7 %placed_30.1 = (f32[4,64,384]{2,1,0:T(8,128)S(1)}, f32[4,64,384]{2,1,0:T(8,128)S(1)}) custom-call(s32[2440]{0:T(1024)S(1)} %concatenate.16.table, f32[1040,128]{1,0:T(8,128)S(1)} %collective-permute-done.10.a_refs_0__0_, f32[1040,128]{1,0:T(8,128)S(1)} %shard_map.57.after_1_.a_refs_1__0_, f32[16384,256]{1,0:T(8,128)} %bitcast.40, ...), custom_call_target="tpu_custom_call" | custom-call | flops 8000000000 | bytes 1310720 | tf_op jit(solution)/shard_map/placed_30/pallas_call | solution.py:194
  103.0 2.2 %collective-permute-start.18 = (f32[4,64,384]{2,1,0:T(8,128)S(1)}, f32[4,64,384]{2,1,0:T(8,128)S(1)}, u32[]{:S(2)}, u32[]{:S(2)}) collective-permute-start(f32[4,64,384]{2,1,0:T(8,128)S(1)} %get-tuple-element.27), channel_id=1, source_target_pairs={{0,16},{8,24},{16,0},{24,8},{1,17},{9,25},{17,1},{25,9},{2,18},{10... | collective-permute-start | bytes 1179656 | tf_op jit(solution)/shard_map/x_30/ppermute | solution.py:450
  105.2 4.7 %placed_31.1 = (f32[4,64,384]{2,1,0:T(8,128)S(1)}, f32[4,64,384]{2,1,0:T(8,128)S(1)}) custom-call(s32[2440]{0:T(1024)S(1)} %concatenate.16.table, f32[1040,128]{1,0:T(8,128)S(1)} %collective-permute-done.9.a_refs_0__0_, f32[1040,128]{1,0:T(8,128)S(1)} %shard_map.58.after_1_.a_refs_1__0_, f32[16384,256]{1,0:T(8,128)} %bitcast.41, ...), custom_call_target="tpu_custom_call" | custom-call | flops 8000000000 | bytes 1310720 | tf_op jit(solution)/shard_map/placed_31/pallas_call | solution.py:194
  111.4 2.8 %collective-permute-done.18.two = f32[4,64,384]{2,1,0:T(8,128)S(1)} collective-permute-done((f32[4,64,384]{2,1,0:T(8,128)S(1)}, f32[4,64,384]{2,1,0:T(8,128)S(1)}, u32[]{:S(2)}, u32[]{:S(2)}) %collective-permute-start.18) | collective-permute-done | bytes 393248 | tf_op jit(solution)/shard_map/x_30/ppermute | solution.py:450
  115.6 3.8 %collective-permute-done.14.two = f32[4,64,384]{2,1,0:T(8,128)S(1)} collective-permute-done((f32[4,64,384]{2,1,0:T(8,128)S(1)}, f32[4,64,384]{2,1,0:T(8,128)S(1)}, u32[]{:S(2)}, u32[]{:S(2)}) %collective-permute-start.14) | collective-permute-done | bytes 393248 | tf_op jit(solution)/shard_map/x_31/ppermute | solution.py:450
  119.4 1.5 %collective-permute-done.16.after_1_.other = f32[4,64,384]{2,1,0:T(8,128)S(1)} collective-permute-done((f32[4,64,384]{2,1,0:T(8,128)S(1)}, f32[4,64,384]{2,1,0:T(8,128)S(1)}, u32[]{:S(2)}, u32[]{:S(2)}) %collective-permute-start.16) | collective-permute-done | bytes 393248 | tf_op jit(solution)/shard_map/y_21/ppermute | solution.py:465
  121.0 4.4 %collective-permute-start.17 = (f32[4,64,384]{2,1,0:T(8,128)S(1)}, f32[4,64,384]{2,1,0:T(8,128)S(1)}, u32[]{:S(2)}, u32[]{:S(2)}) collective-permute-start(f32[4,64,384]{2,1,0:T(8,128)S(1)} %sum_31.1.total), channel_id=1, source_target_pairs={{0,1},{2,3},{5,4},{7,6},{8,9},{10,11},{13,12},{15,14},{16,17},{18,... | collective-permute-start | bytes 1179656 | tf_op jit(solution)/shard_map/y_31/ppermute | solution.py:465
  125.4 1.5 %shard_map.59.refs_0_ = f32[16,1,64,384]{3,2,1,0:T(8,128)} custom-call(s32[4]{0:T(128)S(1)} %pad_add_fusion.meta.table, f32[8,64,384]{2,1,0:T(8,128)S(1)} %sum_00.1.total, f32[8,64,384]{2,1,0:T(8,128)S(1)} %collective-permute-done.12.after_1_.other), custom_call_target="tpu_custom_call" | custom-call | bytes 2359296 | tf_op jit(solution)/shard_map/pallas_call | solution.py:265
  126.9 1.5 %shard_map.60.refs_0_ = f32[16,1,64,384]{3,2,1,0:T(8,128)} custom-call(s32[4]{0:T(128)S(1)} %pad_add_fusion.meta.table, f32[8,64,384]{2,1,0:T(8,128)S(1)} %sum_10.1.total, f32[8,64,384]{2,1,0:T(8,128)S(1)} %collective-permute-done.20.after_1_.other, f32[16,1,64,384]{3,2,1,0:T(8,128)} %shard_map.59.refs_0_), custom_call_target="tpu_custom_call", output_to_operand_aliasing={{}: (3, {})} | custom-call | bytes 2359296 | tf_op jit(solution)/shard_map/pallas_call | solution.py:265
  130.2 4.3 %collective-permute-done.17.other = f32[4,64,384]{2,1,0:T(8,128)S(1)} collective-permute-done((f32[4,64,384]{2,1,0:T(8,128)S(1)}, f32[4,64,384]{2,1,0:T(8,128)S(1)}, u32[]{:S(2)}, u32[]{:S(2)}) %collective-permute-start.17) | collective-permute-done | bytes 393248 | tf_op jit(solution)/shard_map/y_31/ppermute | solution.py:465
  (79 shorter events, 25.3 us)
Async XLA Ops:
  0.0 26.2 %collective-permute-start.5 = (f32[16384,256]{1,0:T(8,128)}, f32[16384,256]{1,0:T(8,128)}, u32[]{:S(2)}, u32[]{:S(2)}) collective-permute-start(f32[16384,256]{1,0:T(8,128)} %bitcast.35), channel_id=1, source_target_pairs={{0,8},{8,0},{16,24},{24,16},{1,9},{9,1},{17,25},{25,17},{2,10},{10... | collective-permute-start | bytes 50331656 | tf_op jit(solution)/shard_map/mate/ppermute | solution.py:369
  4.3 10.8 %collective-permute-start.3 = (f32[520,128]{1,0:T(8,128)S(1)}, f32[520,128]{1,0:T(8,128)S(1)}, u32[]{:S(2)}, u32[]{:S(2)}) collective-permute-start(f32[520,128]{1,0:T(8,128)S(1)} %get-tuple-element.37), channel_id=1, source_target_pairs={{0,17},{1,16},{8,25},{9,24},{16,1},{17,0},{24,9},{25,8},{2,19},{3,... | collective-permute-start | bytes 798728 | tf_op jit(solution)/shard_map/spread_11/ppermute | solution.py:398
  7.8 12.8 %collective-permute-start.2 = (f32[520,128]{1,0:T(8,128)S(1)}, f32[520,128]{1,0:T(8,128)S(1)}, u32[]{:S(2)}, u32[]{:S(2)}) collective-permute-start(f32[520,128]{1,0:T(8,128)S(1)} %get-tuple-element.39), channel_id=1, source_target_pairs={{0,1},{1,0},{8,9},{9,8},{16,17},{17,16},{24,25},{25,24},{2,3},{3,2... | collective-permute-start | bytes 798728 | tf_op jit(solution)/shard_map/spread_01/ppermute | solution.py:398
  8.3 12.6 %collective-permute-start.1 = (f32[520,128]{1,0:T(8,128)S(1)}, f32[520,128]{1,0:T(8,128)S(1)}, u32[]{:S(2)}, u32[]{:S(2)}) collective-permute-start(f32[520,128]{1,0:T(8,128)S(1)} %get-tuple-element.40), channel_id=1, source_target_pairs={{0,16},{1,17},{8,24},{9,25},{16,0},{17,1},{24,8},{25,9},{2,18},{3,... | collective-permute-start | bytes 798728 | tf_op jit(solution)/shard_map/spread_10/ppermute | solution.py:398
  8.7 17.4 %collective-permute-start = (s32[1024]{0:T(1024)S(1)}, s32[1024]{0:T(1024)S(1)}, u32[]{:S(2)}, u32[]{:S(2)}) collective-permute-start(s32[1024]{0:T(1024)S(1)} %reshape.69), channel_id=1, source_target_pairs={{0,8},{8,0},{16,24},{24,16},{1,9},{9,1},{17,25},{25,17},{2,10},{10... | collective-permute-start | bytes 12296 | tf_op jit(solution)/shard_map/mate_index/ppermute | solution.py:371
  21.0 16.7 %collective-permute-start.6 = (f32[2080,128]{1,0:T(8,128)S(1)}, f32[2080,128]{1,0:T(8,128)S(1)}, u32[]{:S(2)}, u32[]{:S(2)}) collective-permute-start(f32[2080,128]{1,0:T(8,128)S(1)} %joined.1.a_refs_0__0_), channel_id=1, source_target_pairs={{2,4},{4,2},{3,5},{5,3},{10,12},{12,10},{11,13},{13,11},{18,20},{2... | collective-permute-start | bytes 3194888 | tf_op jit(solution)/shard_map/inner/ppermute | solution.py:344
  21.8 27.8 %collective-permute-start.4 = (f32[2080,128]{1,0:T(8,128)S(1)}, f32[2080,128]{1,0:T(8,128)}, u32[]{:S(2)}, u32[]{:S(2)}) collective-permute-start(f32[2080,128]{1,0:T(8,128)S(1)} %joined.1.a_refs_0__0_), channel_id=1, source_target_pairs={{0,2},{2,0},{4,6},{6,4},{1,3},{3,1},{5,7},{7,5},{8,10},{10,8},{12,... | collective-permute-start | bytes 3194888 | tf_op jit(solution)/shard_map/near/ppermute | solution.py:344
  35.5 25.6 %collective-permute-start.11 = (f32[8,64,384]{2,1,0:T(8,128)}, f32[8,64,384]{2,1,0:T(8,128)}, u32[]{:S(2)}, u32[]{:S(2)}) collective-permute-start(f32[8,64,384]{2,1,0:T(8,128)} %get-tuple-element.21), channel_id=1, source_target_pairs={{0,16},{8,24},{16,0},{24,8},{1,17},{9,25},{17,1},{25,9},{2,18},{10... | collective-permute-start | bytes 2359304 | tf_op jit(solution)/shard_map/x_00/ppermute | solution.py:450
  38.7 36.6 %collective-permute-start.8 = (f32[2080,128]{1,0:T(8,128)}, f32[2080,128]{1,0:T(8,128)S(1)}, u32[]{:S(2)}, u32[]{:S(2)}) collective-permute-start(f32[2080,128]{1,0:T(8,128)} %shard_map.55.after_1_.a_refs_1__0_), channel_id=1, source_target_pairs={{2,0},{4,6},{3,1},{5,7},{10,8},{12,14},{11,9},{13,15},{18,16},{20,... | collective-permute-start | bytes 3194888 | tf_op jit(solution)/shard_map/outer/ppermute | solution.py:344
  49.6 14.2 %collective-permute-start.7 = (f32[2080,128]{1,0:T(8,128)}, f32[2080,128]{1,0:T(8,128)S(1)}, u32[]{:S(2)}, u32[]{:S(2)}) collective-permute-start(f32[2080,128]{1,0:T(8,128)} %shard_map.56.a_refs_0__0_), channel_id=1, source_target_pairs={{4,2},{2,4},{5,3},{3,5},{12,10},{10,12},{13,11},{11,13},{20,18},{1... | collective-permute-start | bytes 3194888 | tf_op jit(solution)/shard_map/through/ppermute | solution.py:344
  59.6 30.6 %collective-permute-start.19 = (f32[8,64,384]{2,1,0:T(8,128)S(1)}, f32[8,64,384]{2,1,0:T(8,128)S(1)}, u32[]{:S(2)}, u32[]{:S(2)}) collective-permute-start(f32[8,64,384]{2,1,0:T(8,128)S(1)} %get-tuple-element.28), channel_id=1, source_target_pairs={{0,16},{8,24},{16,0},{24,8},{1,17},{9,25},{17,1},{25,9},{2,18},{10... | collective-permute-start | bytes 2359304 | tf_op jit(solution)/shard_map/x_10/ppermute | solution.py:450
  62.4 14.9 %copy-start.1 = (f32[2080,128]{1,0:T(8,128)S(1)}, f32[2080,128]{1,0:T(8,128)}, u32[]{:S(2)}) copy-start(f32[2080,128]{1,0:T(8,128)} %shard_map.55.after_1_.a_refs_1__0_) | copy-start | bytes 3194884
  62.4 31.0 %collective-permute-start.12 = (f32[8,64,384]{2,1,0:T(8,128)S(1)}, f32[8,64,384]{2,1,0:T(8,128)S(1)}, u32[]{:S(2)}, u32[]{:S(2)}) collective-permute-start(f32[8,64,384]{2,1,0:T(8,128)S(1)} %sum_00.1.total), channel_id=1, source_target_pairs={{1,0},{3,2},{4,5},{6,7},{9,8},{11,10},{12,13},{14,15},{17,16},{19,... | collective-permute-start | bytes 2359304 | tf_op jit(solution)/shard_map/y_00/ppermute | solution.py:465
  75.9 22.4 %collective-permute-start.10 = (f32[1040,128]{1,0:T(8,128)S(1)}, f32[1040,128]{1,0:T(8,128)S(1)}, u32[]{:S(2)}, u32[]{:S(2)}) collective-permute-start(f32[1040,128]{1,0:T(8,128)S(1)} %shard_map.57.after_1_.a_refs_1__0_), channel_id=1, source_target_pairs={{2,0},{4,6},{3,1},{5,7},{10,8},{12,14},{11,9},{13,15},{18,16},{20,... | collective-permute-start | bytes 1597448 | tf_op jit(solution)/shard_map/last/ppermute | solution.py:344
  82.0 10.0 %collective-permute-start.13 = (f32[4,64,384]{2,1,0:T(8,128)S(1)}, f32[4,64,384]{2,1,0:T(8,128)S(1)}, u32[]{:S(2)}, u32[]{:S(2)}) collective-permute-start(f32[4,64,384]{2,1,0:T(8,128)S(1)} %get-tuple-element.23), channel_id=1, source_target_pairs={{0,16},{8,24},{16,0},{24,8},{1,17},{9,25},{17,1},{25,9},{2,18},{10... | collective-permute-start | bytes 1179656 | tf_op jit(solution)/shard_map/x_20/ppermute | solution.py:450
  84.2 21.0 %collective-permute-start.9 = (f32[1040,128]{1,0:T(8,128)S(1)}, f32[1040,128]{1,0:T(8,128)S(1)}, u32[]{:S(2)}, u32[]{:S(2)}) collective-permute-start(f32[1040,128]{1,0:T(8,128)S(1)} %shard_map.58.after_1_.a_refs_1__0_), channel_id=1, source_target_pairs={{2,0},{4,6},{3,1},{5,7},{10,8},{12,14},{11,9},{13,15},{18,16},{20,... | collective-permute-start | bytes 1597448 | tf_op jit(solution)/shard_map/last/ppermute | solution.py:344
  90.2 19.8 %collective-permute-start.15 = (f32[4,64,384]{2,1,0:T(8,128)S(1)}, f32[4,64,384]{2,1,0:T(8,128)S(1)}, u32[]{:S(2)}, u32[]{:S(2)}) collective-permute-start(f32[4,64,384]{2,1,0:T(8,128)S(1)} %get-tuple-element.26), channel_id=1, source_target_pairs={{0,16},{8,24},{16,0},{24,8},{1,17},{9,25},{17,1},{25,9},{2,18},{10... | collective-permute-start | bytes 1179656 | tf_op jit(solution)/shard_map/x_21/ppermute | solution.py:450
  92.0 19.4 %collective-permute-start.20 = (f32[8,64,384]{2,1,0:T(8,128)S(1)}, f32[8,64,384]{2,1,0:T(8,128)S(1)}, u32[]{:S(2)}, u32[]{:S(2)}) collective-permute-start(f32[8,64,384]{2,1,0:T(8,128)S(1)} %sum_10.1.total), channel_id=1, source_target_pairs={{1,0},{3,2},{4,5},{6,7},{9,8},{11,10},{12,13},{14,15},{17,16},{19,... | collective-permute-start | bytes 2359304 | tf_op jit(solution)/shard_map/y_10/ppermute | solution.py:465
  93.4 18.0 %collective-permute-start.21 = (f32[4,64,384]{2,1,0:T(8,128)S(1)}, f32[4,64,384]{2,1,0:T(8,128)S(1)}, u32[]{:S(2)}, u32[]{:S(2)}) collective-permute-start(f32[4,64,384]{2,1,0:T(8,128)S(1)} %sum_20.1.after_1_.total), channel_id=1, source_target_pairs={{0,1},{2,3},{5,4},{7,6},{8,9},{10,11},{13,12},{15,14},{16,17},{18,... | collective-permute-start | bytes 1179656 | tf_op jit(solution)/shard_map/y_20/ppermute | solution.py:465
  103.0 11.2 %collective-permute-start.18 = (f32[4,64,384]{2,1,0:T(8,128)S(1)}, f32[4,64,384]{2,1,0:T(8,128)S(1)}, u32[]{:S(2)}, u32[]{:S(2)}) collective-permute-start(f32[4,64,384]{2,1,0:T(8,128)S(1)} %get-tuple-element.27), channel_id=1, source_target_pairs={{0,16},{8,24},{16,0},{24,8},{1,17},{9,25},{17,1},{25,9},{2,18},{10... | collective-permute-start | bytes 1179656 | tf_op jit(solution)/shard_map/x_30/ppermute | solution.py:450
  109.9 9.5 %collective-permute-start.14 = (f32[4,64,384]{2,1,0:T(8,128)S(1)}, f32[4,64,384]{2,1,0:T(8,128)S(1)}, u32[]{:S(2)}, u32[]{:S(2)}) collective-permute-start(f32[4,64,384]{2,1,0:T(8,128)S(1)} %get-tuple-element.25), channel_id=1, source_target_pairs={{0,16},{8,24},{16,0},{24,8},{1,17},{9,25},{17,1},{25,9},{2,18},{10... | collective-permute-start | bytes 1179656 | tf_op jit(solution)/shard_map/x_31/ppermute | solution.py:450
  110.1 10.9 %collective-permute-start.16 = (f32[4,64,384]{2,1,0:T(8,128)S(1)}, f32[4,64,384]{2,1,0:T(8,128)S(1)}, u32[]{:S(2)}, u32[]{:S(2)}) collective-permute-start(f32[4,64,384]{2,1,0:T(8,128)S(1)} %sum_21.1.total), channel_id=1, source_target_pairs={{0,1},{2,3},{5,4},{7,6},{8,9},{10,11},{13,12},{15,14},{16,17},{18,... | collective-permute-start | bytes 1179656 | tf_op jit(solution)/shard_map/y_21/ppermute | solution.py:465
  114.2 15.4 %collective-permute-start.22 = (f32[4,64,384]{2,1,0:T(8,128)S(1)}, f32[4,64,384]{2,1,0:T(8,128)S(1)}, u32[]{:S(2)}, u32[]{:S(2)}) collective-permute-start(f32[4,64,384]{2,1,0:T(8,128)S(1)} %sum_30.1.total), channel_id=1, source_target_pairs={{0,1},{2,3},{5,4},{7,6},{8,9},{10,11},{13,12},{15,14},{16,17},{18,... | collective-permute-start | bytes 1179656 | tf_op jit(solution)/shard_map/y_30/ppermute | solution.py:465
  121.0 13.5 %collective-permute-start.17 = (f32[4,64,384]{2,1,0:T(8,128)S(1)}, f32[4,64,384]{2,1,0:T(8,128)S(1)}, u32[]{:S(2)}, u32[]{:S(2)}) collective-permute-start(f32[4,64,384]{2,1,0:T(8,128)S(1)} %sum_31.1.total), channel_id=1, source_target_pairs={{0,1},{2,3},{5,4},{7,6},{8,9},{10,11},{13,12},{15,14},{16,17},{18,... | collective-permute-start | bytes 1179656 | tf_op jit(solution)/shard_map/y_31/ppermute | solution.py:465
  (4 other events, 17.8 us)

commit v4 on v3

--- a/solution.py
+++ b/solution.py
@@ -274,22 +274,6 @@
     )(meta, total, other, *so_far)
 
 
-def gate_kernel(value, after, out):
-    pass
-
-
-def gated(value, after):
-    anywhere = pl.BlockSpec(memory_space=pl.ANY)
-    return pl.pallas_call(
-        gate_kernel,
-        out_shape=jax.ShapeDtypeStruct(value.shape, value.dtype),
-        in_specs=[anywhere, [anywhere] * len(after)],
-        out_specs=anywhere,
-        input_output_aliases={0: 0},
-        cost_estimate=pl.CostEstimate(flops=0, bytes_accessed=0, transcendentals=0),
-    )(value, after)
-
-
 def sum_kernel(one, two, after, out):
     out[...] = one[...] + two[...]
 
@@ -385,7 +369,7 @@
         return jnp.concatenate([pick(a_by).reshape(-1, LANES), index, c_rows])
 
     own = a_for(0, 0)
-    others = [own]
+    others = []
     for ex in range(halves):
         for e in range(depths):
             if ex or e:
@@ -396,10 +380,11 @@
                 ]
                 with jax.named_scope(f"spread_{ex}{e}"):
                     others.append(lax.ppermute(a_for(ex, e), ("row", "depth"), perm))
-    c_across = others[depths][1 - INDEX_ROWS:].reshape(-1)[:c_index.size].astype(jnp.int32)
+    c_across = others[depths - 1][1 - INDEX_ROWS:].reshape(-1)[:c_index.size].astype(jnp.int32)
+    near_own, inner_own = along(own, "near"), along(own, "inner")
     with jax.named_scope("joined"):
-        here = joined(others, [])
-    near, inner = along(here, "near"), along(here, "inner")
+        rest = joined(others, [near_own, inner_own])
+    near_rest, inner_rest = along(rest, "near"), along(rest, "inner")
     whole_table = jnp.concatenate(
         [jnp.pad(meta, (0, 4)), b_flat, m_flat, c_index.reshape(-1), c_across]
     )
@@ -415,10 +400,10 @@
     number = 0
     for slot in range(tiles):
         if slot == 0:
-            a_sources = [[[here]]]
+            a_sources = [[[own, rest]]]
         elif slot == 1:
-            inner = gated(inner, order)
-            near = gated(near, order + [inner])
+            inner = joined([inner_own, inner_rest], order)
+            near = joined([near_own, near_rest], order + [inner])
             outer, through = along(inner, "outer"), along(near, "through")
             a_sources = [[[near]]]
         elif slot == 2:

time: 137 us -> 127 us (0.927)
  waiting for transfers between devices: 46.5 us -> 38.7 us
  Pallas kernels: 44.6 us -> 41.5 us
  starting transfers between devices: 37.4 us -> 39.9 us
  local copies, waits for them, and re-layouts: 5.91 us -> 4.06 us
    ppermute x3, waiting for transfers between devices: 12 us -> 9.38 us  [on_device(): others.append(lax.ppermute(a_for(ex, e), ('row', 'depth'), perm))]
    ppermute x6 -> x8, starting transfers between devices: 9.84 us -> 12.4 us  [along(): return lax.ppermute(value, 'col', pairs[step])]
    ppermute x6 -> x8, waiting for transfers between devices: 21 us -> 18.8 us  [along(): return lax.ppermute(value, 'col', pairs[step])]
    pallas_call x6, Pallas kernels: 36.5 us -> 34.3 us  [placed_products(): pl.pallas_call(functools.partial(placed_kernel, dims, slot, first, count,...]
    ppermute x6, waiting for transfers between devices: 7.71 us -> 5.62 us  [on_device(): other = lax.ppermute(send, 'row', across)]
    unnamed x13 -> x5, local copies, waits for them, and re-layouts: 3.53 us -> 1.69 us
  transfers between devices with their start and end apart: 23 -> 25, of which waited for: 10 -> 11; matrix products, arithmetic and copies ran while one was open for 3% -> 3% of each run, Pallas kernels for 33% -> 33%
where the time goes in v4:
time: 127 us; the launch traced here: 125 us
  Pallas kernels  41.5 us (33%)
  starting transfers between devices  39.9 us (31%)
  waiting for transfers between devices  38.7 us (30%)
  local copies, waits for them, and re-layouts  4.06 us (3%)
    pallas_call x6, Pallas kernels, placed_products(): pl.pallas_call(functools.partial(placed_kernel, dims, slot, first, count,...  34.3 us
    ppermute x8, waiting for transfers between devices, along(): return lax.ppermute(value, 'col', pairs[step])  18.8 us
    ppermute x6, starting transfers between devices, on_device(): other = lax.ppermute(total, ('col', 'depth'), its_perm)  15.5 us
    ppermute x8, starting transfers between devices, along(): return lax.ppermute(value, 'col', pairs[step])  12.4 us
    ppermute x3, waiting for transfers between devices, on_device(): others.append(lax.ppermute(a_for(ex, e), ('row', 'depth'), perm))  9.38 us
    ppermute x6, starting transfers between devices, on_device(): other = lax.ppermute(send, 'row', across)  7.43 us
    ppermute x6, waiting for transfers between devices, on_device(): other = lax.ppermute(send, 'row', across)  5.62 us
    pallas_call x6, Pallas kernels, settled(): pl.pallas_call(functools.partial(settle_kernel, slot, first, depths, step...  5.3 us
  transfers between devices with their start and end apart: 25, of which 11 were waited for; matrix products, arithmetic and copies ran while one was open for 3% of the time, Pallas kernels for 33%

profile of v4, /device:TPU:0, one launch (start us, length us, event | category | flops | bytes accessed | tf_op | source)
XLA Modules:
  0.0 124.7 jit_solution(688659704145117094)
XLA Ops:
  4.3 3.5 %collective-permute-start.4 = (f32[520,128]{1,0:T(8,128)S(1)}, f32[520,128]{1,0:T(8,128)S(1)}, u32[]{:S(2)}, u32[]{:S(2)}) collective-permute-start(f32[520,128]{1,0:T(8,128)S(1)} %get-tuple-element.37), channel_id=1, source_target_pairs={{0,17},{1,16},{8,25},{9,24},{16,1},{17,0},{24,9},{25,8},{2,19},{3,... | collective-permute-start | bytes 798728 | tf_op jit(solution)/shard_map/spread_11/ppermute | solution.py:382
  9.1 6.0 %collective-permute-done.4.parts_2_ = f32[520,128]{1,0:T(8,128)S(1)} collective-permute-done((f32[520,128]{1,0:T(8,128)S(1)}, f32[520,128]{1,0:T(8,128)S(1)}, u32[]{:S(2)}, u32[]{:S(2)}) %collective-permute-start.4) | collective-permute-done | bytes 266272 | tf_op jit(solution)/shard_map/spread_11/ppermute | solution.py:382
  15.1 2.0 %collective-permute-start.2 = (f32[520,128]{1,0:T(8,128)S(1)}, f32[520,128]{1,0:T(8,128)S(1)}, u32[]{:S(2)}, u32[]{:S(2)}) collective-permute-start(f32[520,128]{1,0:T(8,128)S(1)} %get-tuple-element.38.a_refs_0__0_), channel_id=1, source_target_pairs={{0,2},{2,0},{4,6},{6,4},{1,3},{3,1},{5,7},{7,5},{8,10},{10,8},{12,... | collective-permute-start | bytes 798728 | tf_op jit(solution)/shard_map/near/ppermute | solution.py:328
  17.4 3.2 %collective-permute-done.3.parts_0_ = f32[520,128]{1,0:T(8,128)S(1)} collective-permute-done((f32[520,128]{1,0:T(8,128)S(1)}, f32[520,128]{1,0:T(8,128)S(1)}, u32[]{:S(2)}, u32[]{:S(2)}) %collective-permute-start.3) | collective-permute-done | bytes 266272 | tf_op jit(solution)/shard_map/spread_01/ppermute | solution.py:382
  20.9 2.3 %collective-permute-done.2.after_0_.parts_0_ = f32[520,128]{1,0:T(8,128)S(1)} collective-permute-done((f32[520,128]{1,0:T(8,128)S(1)}, f32[520,128]{1,0:T(8,128)S(1)}, u32[]{:S(2)}, u32[]{:S(2)}) %collective-permute-start.2) | collective-permute-done | bytes 266272 | tf_op jit(solution)/shard_map/near/ppermute | solution.py:328
  24.0 4.4 %collective-permute-start.6 = (f32[1560,128]{1,0:T(8,128)S(1)}, f32[1560,128]{1,0:T(8,128)S(1)}, u32[]{:S(2)}, u32[]{:S(2)}) collective-permute-start(f32[1560,128]{1,0:T(8,128)S(1)} %joined.1.a_refs_0__1_), channel_id=1, source_target_pairs={{0,2},{2,0},{4,6},{6,4},{1,3},{3,1},{5,7},{7,5},{8,10},{10,8},{12,... | collective-permute-start | bytes 2396168 | tf_op jit(solution)/shard_map/near/ppermute | solution.py:328
  28.5 7.7 %placed_00.1 = (f32[8,64,384]{2,1,0:T(8,128)S(1)}, f32[8,64,384]{2,1,0:T(8,128)S(1)}) custom-call(s32[2440]{0:T(1024)S(1)} %concatenate.16.table, f32[520,128]{1,0:T(8,128)S(1)} %get-tuple-element.38.a_refs_0__0_, f32[1560,128]{1,0:T(8,128)S(1)} %joined.1.a_refs_0__1_, f32[16384,256]{1,0:T(8,128)} %bitcast.36, f32[16384,256]{1,0:T(8,128)} %collective-permute-done.7.b_mate), custom_call_target="tpu_custom_call" | custom-call | flops 16000000000 | bytes 2621440 | tf_op jit(solution)/shard_map/placed_00/pallas_call | solution.py:194
  36.2 1.6 %collective-permute-start.13 = (f32[8,64,384]{2,1,0:T(8,128)S(1)}, f32[8,64,384]{2,1,0:T(8,128)S(1)}, u32[]{:S(2)}, u32[]{:S(2)}) collective-permute-start(f32[8,64,384]{2,1,0:T(8,128)S(1)} %get-tuple-element.21), channel_id=1, source_target_pairs={{0,16},{8,24},{16,0},{24,8},{1,17},{9,25},{17,1},{25,9},{2,18},{10... | collective-permute-start | bytes 2359304 | tf_op jit(solution)/shard_map/x_00/ppermute | solution.py:435
  39.2 5.3 %collective-permute-done.6.parts_1_ = f32[1560,128]{1,0:T(8,128)S(1)} collective-permute-done((f32[1560,128]{1,0:T(8,128)S(1)}, f32[1560,128]{1,0:T(8,128)S(1)}, u32[]{:S(2)}, u32[]{:S(2)}) %collective-permute-start.6) | collective-permute-done | bytes 798752 | tf_op jit(solution)/shard_map/near/ppermute | solution.py:328
  45.3 7.7 %placed_10.1 = (f32[8,64,384]{2,1,0:T(8,128)S(1)}, f32[8,64,384]{2,1,0:T(8,128)S(1)}) custom-call(s32[2440]{0:T(1024)S(1)} %concatenate.16.table, f32[2080,128]{1,0:T(8,128)S(1)} %shard_map.56.a_refs_0__0_, f32[16384,256]{1,0:T(8,128)} %bitcast.37, f32[16384,256]{1,0:T(8,128)} %collective-permute-done.7.b_mate, f32[8,64,384]{2,1,0:T(8,128)S(1)} %get-tuple-element.17.after_0_.one), custom_call_target="tpu_custom_call" | custom-call | flops 16000000000 | bytes 2621440 | tf_op jit(solution)/shard_map/placed_10/pallas_call | solution.py:194
  53.1 1.6 %collective-permute-start.21 = (f32[8,64,384]{2,1,0:T(8,128)S(1)}, f32[8,64,384]{2,1,0:T(8,128)S(1)}, u32[]{:S(2)}, u32[]{:S(2)}) collective-permute-start(f32[8,64,384]{2,1,0:T(8,128)S(1)} %get-tuple-element.28), channel_id=1, source_target_pairs={{0,16},{8,24},{16,0},{24,8},{1,17},{9,25},{17,1},{25,9},{2,18},{10... | collective-permute-start | bytes 2359304 | tf_op jit(solution)/shard_map/x_10/ppermute | solution.py:435
  56.2 11.2 %collective-permute-done.10.after_1_.a_refs_0__0_ = f32[2080,128]{1,0:T(8,128)S(1)} collective-permute-done((f32[2080,128]{1,0:T(8,128)S(1)}, f32[2080,128]{1,0:T(8,128)S(1)}, u32[]{:S(2)}, u32[]{:S(2)}) %collective-permute-start.10) | collective-permute-done | bytes 1064992 | tf_op jit(solution)/shard_map/outer/ppermute | solution.py:328
  69.3 4.7 %placed_20.1 = (f32[4,64,384]{2,1,0:T(8,128)S(1)}, f32[4,64,384]{2,1,0:T(8,128)S(1)}) custom-call(s32[2440]{0:T(1024)S(1)} %concatenate.16.table, f32[2080,128]{1,0:T(8,128)S(1)} %collective-permute-done.10.after_1_.a_refs_0__0_, f32[2080,128]{1,0:T(8,128)S(1)} %shard_map.55.after_1_.a_refs_1__0_, f32[16384,256]{1,0:T(8,128)} %bitcast.38, ...), custom_call_target="tpu_custom_call" | custom-call | flops 8000000000 | bytes 1835008 | tf_op jit(solution)/shard_map/placed_20/pallas_call | solution.py:194
  77.6 4.8 %placed_21.1 = (f32[4,64,384]{2,1,0:T(8,128)S(1)}, f32[4,64,384]{2,1,0:T(8,128)S(1)}) custom-call(s32[2440]{0:T(1024)S(1)} %concatenate.16.table, f32[2080,128]{1,0:T(8,128)S(1)} %collective-permute-done.10.after_1_.a_refs_0__0_, f32[2080,128]{1,0:T(8,128)S(1)} %shard_map.55.after_1_.a_refs_1__0_, f32[16384,256]{1,0:T(8,128)} %bitcast.39, ...), custom_call_target="tpu_custom_call" | custom-call | flops 8000000000 | bytes 1835008 | tf_op jit(solution)/shard_map/placed_21/pallas_call | solution.py:194
  84.4 4.6 %collective-permute-start.23 = (f32[4,64,384]{2,1,0:T(8,128)S(1)}, f32[4,64,384]{2,1,0:T(8,128)S(1)}, u32[]{:S(2)}, u32[]{:S(2)}) collective-permute-start(f32[4,64,384]{2,1,0:T(8,128)S(1)} %sum_20.1.after_1_.total), channel_id=1, source_target_pairs={{0,1},{2,3},{5,4},{7,6},{8,9},{10,11},{13,12},{15,14},{16,17},{18,... | collective-permute-start | bytes 1179656 | tf_op jit(solution)/shard_map/y_20/ppermute | solution.py:450
  89.0 4.7 %placed_30.1 = (f32[4,64,384]{2,1,0:T(8,128)S(1)}, f32[4,64,384]{2,1,0:T(8,128)S(1)}) custom-call(s32[2440]{0:T(1024)S(1)} %concatenate.16.table, f32[1040,128]{1,0:T(8,128)S(1)} %collective-permute-done.12.a_refs_0__0_, f32[1040,128]{1,0:T(8,128)S(1)} %shard_map.57.after_1_.a_refs_1__0_, f32[16384,256]{1,0:T(8,128)} %bitcast.40, ...), custom_call_target="tpu_custom_call" | custom-call | flops 8000000000 | bytes 1310720 | tf_op jit(solution)/shard_map/placed_30/pallas_call | solution.py:194
  93.7 1.9 %collective-permute-start.20 = (f32[4,64,384]{2,1,0:T(8,128)S(1)}, f32[4,64,384]{2,1,0:T(8,128)S(1)}, u32[]{:S(2)}, u32[]{:S(2)}) collective-permute-start(f32[4,64,384]{2,1,0:T(8,128)S(1)} %get-tuple-element.27), channel_id=1, source_target_pairs={{0,16},{8,24},{16,0},{24,8},{1,17},{9,25},{17,1},{25,9},{2,18},{10... | collective-permute-start | bytes 1179656 | tf_op jit(solution)/shard_map/x_30/ppermute | solution.py:435
  95.6 4.7 %placed_31.1 = (f32[4,64,384]{2,1,0:T(8,128)S(1)}, f32[4,64,384]{2,1,0:T(8,128)S(1)}) custom-call(s32[2440]{0:T(1024)S(1)} %concatenate.16.table, f32[1040,128]{1,0:T(8,128)S(1)} %collective-permute-done.11.a_refs_0__0_, f32[1040,128]{1,0:T(8,128)S(1)} %shard_map.58.after_1_.a_refs_1__0_, f32[16384,256]{1,0:T(8,128)} %bitcast.41, ...), custom_call_target="tpu_custom_call" | custom-call | flops 8000000000 | bytes 1310720 | tf_op jit(solution)/shard_map/placed_31/pallas_call | solution.py:194
  100.6 2.6 %collective-permute-start.18 = (f32[4,64,384]{2,1,0:T(8,128)S(1)}, f32[4,64,384]{2,1,0:T(8,128)S(1)}, u32[]{:S(2)}, u32[]{:S(2)}) collective-permute-start(f32[4,64,384]{2,1,0:T(8,128)S(1)} %sum_21.1.total), channel_id=1, source_target_pairs={{0,1},{2,3},{5,4},{7,6},{8,9},{10,11},{13,12},{15,14},{16,17},{18,... | collective-permute-start | bytes 1179656 | tf_op jit(solution)/shard_map/y_21/ppermute | solution.py:450
  103.2 1.9 %collective-permute-done.20.two = f32[4,64,384]{2,1,0:T(8,128)S(1)} collective-permute-done((f32[4,64,384]{2,1,0:T(8,128)S(1)}, f32[4,64,384]{2,1,0:T(8,128)S(1)}, u32[]{:S(2)}, u32[]{:S(2)}) %collective-permute-start.20) | collective-permute-done | bytes 393248 | tf_op jit(solution)/shard_map/x_30/ppermute | solution.py:435
  106.4 3.5 %collective-permute-done.16.two = f32[4,64,384]{2,1,0:T(8,128)S(1)} collective-permute-done((f32[4,64,384]{2,1,0:T(8,128)S(1)}, f32[4,64,384]{2,1,0:T(8,128)S(1)}, u32[]{:S(2)}, u32[]{:S(2)}) %collective-permute-start.16) | collective-permute-done | bytes 393248 | tf_op jit(solution)/shard_map/x_31/ppermute | solution.py:435
  110.0 2.7 %collective-permute-done.18.after_1_.other = f32[4,64,384]{2,1,0:T(8,128)S(1)} collective-permute-done((f32[4,64,384]{2,1,0:T(8,128)S(1)}, f32[4,64,384]{2,1,0:T(8,128)S(1)}, u32[]{:S(2)}, u32[]{:S(2)}) %collective-permute-start.18) | collective-permute-done | bytes 393248 | tf_op jit(solution)/shard_map/y_21/ppermute | solution.py:450
  112.8 4.4 %collective-permute-start.19 = (f32[4,64,384]{2,1,0:T(8,128)S(1)}, f32[4,64,384]{2,1,0:T(8,128)S(1)}, u32[]{:S(2)}, u32[]{:S(2)}) collective-permute-start(f32[4,64,384]{2,1,0:T(8,128)S(1)} %sum_31.1.total), channel_id=1, source_target_pairs={{0,1},{2,3},{5,4},{7,6},{8,9},{10,11},{13,12},{15,14},{16,17},{18,... | collective-permute-start | bytes 1179656 | tf_op jit(solution)/shard_map/y_31/ppermute | solution.py:450
  122.0 2.2 %collective-permute-done.19.other = f32[4,64,384]{2,1,0:T(8,128)S(1)} collective-permute-done((f32[4,64,384]{2,1,0:T(8,128)S(1)}, f32[4,64,384]{2,1,0:T(8,128)S(1)}, u32[]{:S(2)}, u32[]{:S(2)}) %collective-permute-start.19) | collective-permute-done | bytes 393248 | tf_op jit(solution)/shard_map/y_31/ppermute | solution.py:450
  (75 shorter events, 25.3 us)
Async XLA Ops:
  0.0 28.5 %collective-permute-start.7 = (f32[16384,256]{1,0:T(8,128)}, f32[16384,256]{1,0:T(8,128)}, u32[]{:S(2)}, u32[]{:S(2)}) collective-permute-start(f32[16384,256]{1,0:T(8,128)} %bitcast.35), channel_id=1, source_target_pairs={{0,8},{8,0},{16,24},{24,16},{1,9},{9,1},{17,25},{25,17},{2,10},{10... | collective-permute-start | bytes 50331656 | tf_op jit(solution)/shard_map/mate/ppermute | solution.py:353
  4.3 10.8 %collective-permute-start.4 = (f32[520,128]{1,0:T(8,128)S(1)}, f32[520,128]{1,0:T(8,128)S(1)}, u32[]{:S(2)}, u32[]{:S(2)}) collective-permute-start(f32[520,128]{1,0:T(8,128)S(1)} %get-tuple-element.37), channel_id=1, source_target_pairs={{0,17},{1,16},{8,25},{9,24},{16,1},{17,0},{24,9},{25,8},{2,19},{3,... | collective-permute-start | bytes 798728 | tf_op jit(solution)/shard_map/spread_11/ppermute | solution.py:382
  7.8 12.8 %collective-permute-start.3 = (f32[520,128]{1,0:T(8,128)S(1)}, f32[520,128]{1,0:T(8,128)S(1)}, u32[]{:S(2)}, u32[]{:S(2)}) collective-permute-start(f32[520,128]{1,0:T(8,128)S(1)} %get-tuple-element.39), channel_id=1, source_target_pairs={{0,1},{1,0},{8,9},{9,8},{16,17},{17,16},{24,25},{25,24},{2,3},{3,2... | collective-permute-start | bytes 798728 | tf_op jit(solution)/shard_map/spread_01/ppermute | solution.py:382
  8.3 12.6 %collective-permute-start.1 = (f32[520,128]{1,0:T(8,128)S(1)}, f32[520,128]{1,0:T(8,128)S(1)}, u32[]{:S(2)}, u32[]{:S(2)}) collective-permute-start(f32[520,128]{1,0:T(8,128)S(1)} %get-tuple-element.40), channel_id=1, source_target_pairs={{0,16},{1,17},{8,24},{9,25},{16,0},{17,1},{24,8},{25,9},{2,18},{3,... | collective-permute-start | bytes 798728 | tf_op jit(solution)/shard_map/spread_10/ppermute | solution.py:382
  8.5 12.4 %collective-permute-start.5 = (f32[520,128]{1,0:T(8,128)S(1)}, f32[520,128]{1,0:T(8,128)S(1)}, u32[]{:S(2)}, u32[]{:S(2)}) collective-permute-start(f32[520,128]{1,0:T(8,128)S(1)} %get-tuple-element.38.a_refs_0__0_), channel_id=1, source_target_pairs={{2,4},{4,2},{3,5},{5,3},{10,12},{12,10},{11,13},{13,11},{18,20},{2... | collective-permute-start | bytes 798728 | tf_op jit(solution)/shard_map/inner/ppermute | solution.py:328
  15.1 8.0 %collective-permute-start.2 = (f32[520,128]{1,0:T(8,128)S(1)}, f32[520,128]{1,0:T(8,128)S(1)}, u32[]{:S(2)}, u32[]{:S(2)}) collective-permute-start(f32[520,128]{1,0:T(8,128)S(1)} %get-tuple-element.38.a_refs_0__0_), channel_id=1, source_target_pairs={{0,2},{2,0},{4,6},{6,4},{1,3},{3,1},{5,7},{7,5},{8,10},{10,8},{12,... | collective-permute-start | bytes 798728 | tf_op jit(solution)/shard_map/near/ppermute | solution.py:328
  23.3 14.5 %collective-permute-start.8 = (f32[1560,128]{1,0:T(8,128)S(1)}, f32[1560,128]{1,0:T(8,128)S(1)}, u32[]{:S(2)}, u32[]{:S(2)}) collective-permute-start(f32[1560,128]{1,0:T(8,128)S(1)} %joined.1.a_refs_0__1_), channel_id=1, source_target_pairs={{2,4},{4,2},{3,5},{5,3},{10,12},{12,10},{11,13},{13,11},{18,20},{2... | collective-permute-start | bytes 2396168 | tf_op jit(solution)/shard_map/inner/ppermute | solution.py:328
  24.0 20.5 %collective-permute-start.6 = (f32[1560,128]{1,0:T(8,128)S(1)}, f32[1560,128]{1,0:T(8,128)S(1)}, u32[]{:S(2)}, u32[]{:S(2)}) collective-permute-start(f32[1560,128]{1,0:T(8,128)S(1)} %joined.1.a_refs_0__1_), channel_id=1, source_target_pairs={{0,2},{2,0},{4,6},{6,4},{1,3},{3,1},{5,7},{7,5},{8,10},{10,8},{12,... | collective-permute-start | bytes 2396168 | tf_op jit(solution)/shard_map/near/ppermute | solution.py:328
  36.2 18.6 %collective-permute-start.13 = (f32[8,64,384]{2,1,0:T(8,128)S(1)}, f32[8,64,384]{2,1,0:T(8,128)S(1)}, u32[]{:S(2)}, u32[]{:S(2)}) collective-permute-start(f32[8,64,384]{2,1,0:T(8,128)S(1)} %get-tuple-element.21), channel_id=1, source_target_pairs={{0,16},{8,24},{16,0},{24,8},{1,17},{9,25},{17,1},{25,9},{2,18},{10... | collective-permute-start | bytes 2359304 | tf_op jit(solution)/shard_map/x_00/ppermute | solution.py:435
  37.9 29.5 %collective-permute-start.10 = (f32[2080,128]{1,0:T(8,128)S(1)}, f32[2080,128]{1,0:T(8,128)S(1)}, u32[]{:S(2)}, u32[]{:S(2)}) collective-permute-start(f32[2080,128]{1,0:T(8,128)S(1)} %shard_map.55.after_1_.a_refs_1__0_), channel_id=1, source_target_pairs={{2,0},{4,6},{3,1},{5,7},{10,8},{12,14},{11,9},{13,15},{18,16},{20,... | collective-permute-start | bytes 3194888 | tf_op jit(solution)/shard_map/outer/ppermute | solution.py:328
  44.6 11.6 %collective-permute-start.9 = (f32[2080,128]{1,0:T(8,128)S(1)}, f32[2080,128]{1,0:T(8,128)S(1)}, u32[]{:S(2)}, u32[]{:S(2)}) collective-permute-start(f32[2080,128]{1,0:T(8,128)S(1)} %shard_map.56.a_refs_0__0_), channel_id=1, source_target_pairs={{4,2},{2,4},{5,3},{3,5},{12,10},{10,12},{13,11},{11,13},{20,18},{1... | collective-permute-start | bytes 3194888 | tf_op jit(solution)/shard_map/through/ppermute | solution.py:328
  53.1 29.3 %collective-permute-start.21 = (f32[8,64,384]{2,1,0:T(8,128)S(1)}, f32[8,64,384]{2,1,0:T(8,128)S(1)}, u32[]{:S(2)}, u32[]{:S(2)}) collective-permute-start(f32[8,64,384]{2,1,0:T(8,128)S(1)} %get-tuple-element.28), channel_id=1, source_target_pairs={{0,16},{8,24},{16,0},{24,8},{1,17},{9,25},{17,1},{25,9},{2,18},{10... | collective-permute-start | bytes 2359304 | tf_op jit(solution)/shard_map/x_10/ppermute | solution.py:435
  54.9 29.5 %collective-permute-start.14 = (f32[8,64,384]{2,1,0:T(8,128)S(1)}, f32[8,64,384]{2,1,0:T(8,128)S(1)}, u32[]{:S(2)}, u32[]{:S(2)}) collective-permute-start(f32[8,64,384]{2,1,0:T(8,128)S(1)} %sum_00.1.total), channel_id=1, source_target_pairs={{1,0},{3,2},{4,5},{6,7},{9,8},{11,10},{12,13},{14,15},{17,16},{19,... | collective-permute-start | bytes 2359304 | tf_op jit(solution)/shard_map/y_00/ppermute | solution.py:450
  68.0 21.0 %collective-permute-start.12 = (f32[1040,128]{1,0:T(8,128)S(1)}, f32[1040,128]{1,0:T(8,128)S(1)}, u32[]{:S(2)}, u32[]{:S(2)}) collective-permute-start(f32[1040,128]{1,0:T(8,128)S(1)} %shard_map.57.after_1_.a_refs_1__0_), channel_id=1, source_target_pairs={{2,0},{4,6},{3,1},{5,7},{10,8},{12,14},{11,9},{13,15},{18,16},{20,... | collective-permute-start | bytes 1597448 | tf_op jit(solution)/shard_map/last/ppermute | solution.py:328
  74.1 8.9 %collective-permute-start.15 = (f32[4,64,384]{2,1,0:T(8,128)S(1)}, f32[4,64,384]{2,1,0:T(8,128)S(1)}, u32[]{:S(2)}, u32[]{:S(2)}) collective-permute-start(f32[4,64,384]{2,1,0:T(8,128)S(1)} %get-tuple-element.23), channel_id=1, source_target_pairs={{0,16},{8,24},{16,0},{24,8},{1,17},{9,25},{17,1},{25,9},{2,18},{10... | collective-permute-start | bytes 1179656 | tf_op jit(solution)/shard_map/x_20/ppermute | solution.py:435
  76.3 19.3 %collective-permute-start.11 = (f32[1040,128]{1,0:T(8,128)S(1)}, f32[1040,128]{1,0:T(8,128)S(1)}, u32[]{:S(2)}, u32[]{:S(2)}) collective-permute-start(f32[1040,128]{1,0:T(8,128)S(1)} %shard_map.58.after_1_.a_refs_1__0_), channel_id=1, source_target_pairs={{2,0},{4,6},{3,1},{5,7},{10,8},{12,14},{11,9},{13,15},{18,16},{20,... | collective-permute-start | bytes 1597448 | tf_op jit(solution)/shard_map/last/ppermute | solution.py:328
  82.3 18.2 %collective-permute-start.17 = (f32[4,64,384]{2,1,0:T(8,128)S(1)}, f32[4,64,384]{2,1,0:T(8,128)S(1)}, u32[]{:S(2)}, u32[]{:S(2)}) collective-permute-start(f32[4,64,384]{2,1,0:T(8,128)S(1)} %get-tuple-element.26), channel_id=1, source_target_pairs={{0,16},{8,24},{16,0},{24,8},{1,17},{9,25},{17,1},{25,9},{2,18},{10... | collective-permute-start | bytes 1179656 | tf_op jit(solution)/shard_map/x_21/ppermute | solution.py:435
  83.0 20.2 %collective-permute-start.22 = (f32[8,64,384]{2,1,0:T(8,128)S(1)}, f32[8,64,384]{2,1,0:T(8,128)S(1)}, u32[]{:S(2)}, u32[]{:S(2)}) collective-permute-start(f32[8,64,384]{2,1,0:T(8,128)S(1)} %sum_10.1.total), channel_id=1, source_target_pairs={{1,0},{3,2},{4,5},{6,7},{9,8},{11,10},{12,13},{14,15},{17,16},{19,... | collective-permute-start | bytes 2359304 | tf_op jit(solution)/shard_map/y_10/ppermute | solution.py:450
  84.4 18.8 %collective-permute-start.23 = (f32[4,64,384]{2,1,0:T(8,128)S(1)}, f32[4,64,384]{2,1,0:T(8,128)S(1)}, u32[]{:S(2)}, u32[]{:S(2)}) collective-permute-start(f32[4,64,384]{2,1,0:T(8,128)S(1)} %sum_20.1.after_1_.total), channel_id=1, source_target_pairs={{0,1},{2,3},{5,4},{7,6},{8,9},{10,11},{13,12},{15,14},{16,17},{18,... | collective-permute-start | bytes 1179656 | tf_op jit(solution)/shard_map/y_20/ppermute | solution.py:450
  93.7 11.4 %collective-permute-start.20 = (f32[4,64,384]{2,1,0:T(8,128)S(1)}, f32[4,64,384]{2,1,0:T(8,128)S(1)}, u32[]{:S(2)}, u32[]{:S(2)}) collective-permute-start(f32[4,64,384]{2,1,0:T(8,128)S(1)} %get-tuple-element.27), channel_id=1, source_target_pairs={{0,16},{8,24},{16,0},{24,8},{1,17},{9,25},{17,1},{25,9},{2,18},{10... | collective-permute-start | bytes 1179656 | tf_op jit(solution)/shard_map/x_30/ppermute | solution.py:435
  100.3 9.7 %collective-permute-start.16 = (f32[4,64,384]{2,1,0:T(8,128)S(1)}, f32[4,64,384]{2,1,0:T(8,128)S(1)}, u32[]{:S(2)}, u32[]{:S(2)}) collective-permute-start(f32[4,64,384]{2,1,0:T(8,128)S(1)} %get-tuple-element.25), channel_id=1, source_target_pairs={{0,16},{8,24},{16,0},{24,8},{1,17},{9,25},{17,1},{25,9},{2,18},{10... | collective-permute-start | bytes 1179656 | tf_op jit(solution)/shard_map/x_31/ppermute | solution.py:435
  100.6 12.1 %collective-permute-start.18 = (f32[4,64,384]{2,1,0:T(8,128)S(1)}, f32[4,64,384]{2,1,0:T(8,128)S(1)}, u32[]{:S(2)}, u32[]{:S(2)}) collective-permute-start(f32[4,64,384]{2,1,0:T(8,128)S(1)} %sum_21.1.total), channel_id=1, source_target_pairs={{0,1},{2,3},{5,4},{7,6},{8,9},{10,11},{13,12},{15,14},{16,17},{18,... | collective-permute-start | bytes 1179656 | tf_op jit(solution)/shard_map/y_21/ppermute | solution.py:450
  105.1 16.3 %collective-permute-start.24 = (f32[4,64,384]{2,1,0:T(8,128)S(1)}, f32[4,64,384]{2,1,0:T(8,128)S(1)}, u32[]{:S(2)}, u32[]{:S(2)}) collective-permute-start(f32[4,64,384]{2,1,0:T(8,128)S(1)} %sum_30.1.total), channel_id=1, source_target_pairs={{0,1},{2,3},{5,4},{7,6},{8,9},{10,11},{13,12},{15,14},{16,17},{18,... | collective-permute-start | bytes 1179656 | tf_op jit(solution)/shard_map/y_30/ppermute | solution.py:450
  112.8 11.4 %collective-permute-start.19 = (f32[4,64,384]{2,1,0:T(8,128)S(1)}, f32[4,64,384]{2,1,0:T(8,128)S(1)}, u32[]{:S(2)}, u32[]{:S(2)}) collective-permute-start(f32[4,64,384]{2,1,0:T(8,128)S(1)} %sum_31.1.total), channel_id=1, source_target_pairs={{0,1},{2,3},{5,4},{7,6},{8,9},{10,11},{13,12},{15,14},{16,17},{18,... | collective-permute-start | bytes 1179656 | tf_op jit(solution)/shard_map/y_31/ppermute | solution.py:450
  (2 other events, 20.8 us)
